TPU v7x, 128 devices: a whole 4x4x4 slice. The times are simulated.
128 devices in a mesh: cluster: 8 (over y, z_hi), col: 2 (over core), blk: 8 (over z_lo, x).
Axes of the slice: x: 4, y: 4, z: 4 (z_hi: 2, z_lo: 2; z = z_hi * 2 + z_lo), core: 2. Of those that a mesh axis runs over, the one named last changes fastest.
Arguments:
- embeddings: bfloat16 [49152, 512], P(('cluster', 'col', 'blk')), may hold values from -6 to 6
- assignment: int32 [49152, 1], P(('cluster', 'col', 'blk')), may hold values from 0 to 7; in each aligned block of 384 rows (0 to 383, 384 to 767, ...) at most 128 rows name the same one
Outputs:
- best_similarity: float32 [49152], P(('cluster', 'col', 'blk'))
Inputs may be any that keep to these rules, and one draw needn't show every extreme that they name: `assignment`: within the rows of one device no cluster is named more than 128 times; some cluster is named exactly 128 times in some or all devices, and every cluster is named by two or more rows in all.
All inputs are finite; a program needn't handle non-finite values.
Results may differ from a plain program's by a relative error of at most 0.0012.
Values may be sent and summed in bfloat16 or wider, within the bound.
A program may use at most 64 MiB of HBM per device.

v0:
```python
import math

import jax
import jax.numpy as jnp
from jax import lax
from jax.sharding import PartitionSpec as P

CAP = 128


def normalize(embeddings):
    values = embeddings.astype(jnp.float32)
    features = embeddings.shape[1]
    scaled = (
        values
        * lax.rsqrt(jnp.mean(values * values, axis=-1, keepdims=True) + 1e-06)
        / math.sqrt(features)
    )
    return scaled.astype(jnp.bfloat16)


def fold_rows(row_data, row_numbers, column_data, occupied, column_numbers):
    total = row_data.shape[0]
    row_step = math.gcd(512, total)
    block_count = total // row_step

    def one_block(block_args):
        row_piece, piece_numbers = block_args
        scores = jnp.einsum("rd,cd->rc", row_piece, column_data, preferred_element_type=jnp.float32)
        allowed = (occupied[None, :] > 0) & (piece_numbers[:, None] != column_numbers[None, :])
        return jnp.max(jnp.where(allowed, scores, -jnp.inf), axis=1)

    fresh = lax.map(
        one_block,
        (row_data.reshape(block_count, row_step, -1), row_numbers.reshape(block_count, row_step)),
    )
    return fresh.reshape(total)


def local(embeddings, assignment):
    features = embeddings.shape[1]
    groups = lax.axis_size("cluster")
    blk_count = lax.axis_size("blk")
    slots = groups * CAP
    unit_rows = normalize(embeddings)
    cluster_ids = assignment[:, 0]
    onehot = (cluster_ids[:, None] == jnp.arange(groups, dtype=jnp.int32)[None, :]).astype(
        jnp.int32
    )
    earlier = jnp.cumsum(onehot, axis=0) - onehot
    slot_index = jnp.sum(earlier * onehot, axis=1)
    target = cluster_ids * CAP + slot_index
    buffer = jnp.zeros((slots, features), jnp.bfloat16).at[target].set(unit_rows)
    filled = (
        jnp.zeros((slots,), jnp.bfloat16).at[target].set(jnp.ones((target.shape[0],), jnp.bfloat16))
    )
    members, occupied = (
        lax.all_to_all(
            buffer.reshape(groups, CAP, features),
            "cluster",
            split_axis=0,
            concat_axis=0,
            tiled=True,
        ),
        lax.all_to_all(
            filled.reshape(groups, CAP), "cluster", split_axis=0, concat_axis=0, tiled=True
        ),
    )
    members = members.reshape(slots, features)
    occupied = occupied.reshape(slots)
    col_here = lax.axis_index("col")
    blk_here = lax.axis_index("blk")
    own_numbers = (col_here * blk_count + blk_here) * slots + jnp.arange(slots, dtype=jnp.int32)
    column_data = lax.all_gather(members, ("col", "blk"), axis=0, tiled=True)
    column_occupied = lax.all_gather(occupied, ("col", "blk"), axis=0, tiled=True)
    column_numbers = jnp.arange(column_data.shape[0], dtype=jnp.int32)
    own_best = fold_rows(members, own_numbers, column_data, column_occupied, column_numbers)
    returned = lax.all_to_all(
        own_best.reshape(groups, CAP), "cluster", split_axis=0, concat_axis=0, tiled=True
    )
    return returned.reshape(slots)[target]


def solution(mesh):
    in_specs = (P(("cluster", "col", "blk"), None), P(("cluster", "col", "blk"), None))
    out_specs = P(("cluster", "col", "blk"))
    return jax.shard_map(local, mesh=mesh, in_specs=in_specs, out_specs=out_specs, check_vma=False)
```

profile of v0, /device:TPU:1, one launch (start us, length us, event | category | flops | bytes accessed | tf_op | source)
XLA Modules:
  0.0 182.0 jit_solution(14505268197120601457)
XLA Ops:
  6.5 0.0 all-gather.2.cloned.1.call-start
  6.5 0.7 reduce
  7.2 0.9 reduce-window.6
  8.1 0.2 slice_reduce_fusion
  8.4 0.1 fusion.15
  8.5 0.7 fusion.17
  9.2 1.2 fusion.6
  10.3 2.8 %scatter_custom_fusion.1 = bf16[1024,512]{1,0:T(8,128)(2,1)S(1)} fusion(s32[384]{0:T(512)S(1)} %fusion.17, bf16[]{:T(256)} %constant.26.clone.1, bf16[384,512]{1,0:T(8,128)(2,1)} %param.4, f32[]{:T(128)} %constant.31.clone.1, f32[384]{0:T(512)S(1)} %add_rsqrt_fusion), kind=kCustom, calls=%fused_computation.17 | custom fusion | flops 786432 | bytes 1443846 | tf_op jit(solution)/shard_map/scatter | solution.py:53
  13.2 23.5 %all_to_all.23 = bf16[8,128,512]{2,1,0:T(8,128)(2,1)} all-to-all(bf16[8,128,512]{2,1,0:T(8,128)(2,1)S(1)} %bitcast.33), channel_id=1, replica_groups=mesh['cluster'=8,'col'=2,'blk'=8] {'cluster'}, dimensions={0} | all-to-all | bytes 2097152 | tf_op jit(solution)/shard_map/all_to_all | solution.py:58
  36.7 0.0 all-gather.2.cloned.1.call-update
  36.7 3.0 %scatter_custom_fusion = bf16[1024]{0:T(1024)(128)(2,1)S(1)} fusion(s32[384]{0:T(512)S(1)} %fusion.17, bf16[384]{0:T(512)(128)(2,1)S(1)} %broadcast.51, bf16[]{:T(256)} %constant.26.clone.1), kind=kCustom, calls=%fused_computation.33 | custom fusion | bytes 2050 | tf_op jit(solution)/shard_map/scatter | solution.py:55
  39.7 0.6 copy.3
  40.3 3.6 %all-to-all-start = ((bf16[8,1,128]{2,1,0:T(2,128)(2,1)}), bf16[8,1,128]{2,1,0:T(2,128)(2,1)S(1)}, u32[]{:S(2)}, u32[]{:S(2)}) async-start(bf16[8,1,128]{2,1,0:T(2,128)(2,1)} %copy.3), calls=%async_computation | async-start | bytes 8192 | tf_op jit(solution)/shard_map/all_to_all | solution.py:65
  43.9 6.3 %all-to-all-done = bf16[8,1,128]{2,1,0:T(2,128)(2,1)S(1)} async-done(((bf16[8,1,128]{2,1,0:T(2,128)(2,1)}), bf16[8,1,128]{2,1,0:T(2,128)(2,1)S(1)}, u32[]{:S(2)}, u32[]{:S(2)}) %all-to-all-start) | async-done | bytes 2080 | tf_op jit(solution)/shard_map/all_to_all | solution.py:65
  50.2 33.2 %all_gather.6 = bf16[16384]{0:T(1024)(128)(2,1)S(1)} all-gather(bf16[1024]{0:T(1024)(128)(2,1)S(1)} %bitcast.39), channel_id=1, replica_groups=mesh['cluster'=8,'col'=2,'blk'=8] {'col','blk'}, dimensions={0}, use_global_device_ids=true | all-gather | bytes 34816 | tf_op jit(solution)/shard_map/all_gather | solution.py:75
  83.4 45.6 %all-gather.2.cloned.1.call-done = bf16[16384,512]{1,0:T(8,128)(2,1)} async-done(((bf16[1024,512]{1,0:T(8,128)(2,1)}), bf16[16384,512]{1,0:T(8,128)(2,1)}) %all-gather.2.cloned.1.call-update) | async-done | bytes 16777232 | tf_op jit(solution)/shard_map/all_gather | solution.py:74
  129.0 29.8 %while.11 = (s32[]{:T(128)}, f32[2,512]{1,0:T(2,128)S(1)}, bf16[16384]{0:T(1024)(128)(2,1)S(1)}, s32[2,512]{1,0:T(2,128)S(1)}, bf16[2,512,512]{2,1,0:T(8,128)(2,...) while((s32[]{:T(128)}, f32[2,512]{1,0:T(2,128)S(1)}, bf16[16384]{0:T(1024)(128)(2,1)S(1)}, ...), condition=%wide.region_8.9_spmd.clone, body=%wide.region_6.8_spmd.clone.sunk | while | flops 8623505408 | bytes 17379932 | solution.py:33
  129.0 14.8 %select_reduce_fusion.2 = f32[512]{0:T(512)S(1)} fusion(bf16[16384,512]{1,0:T(8,128)(2,1)} %get-tuple-element.127, s32[512]{0:T(512)S(1)} %bitcast.35, pred[16384]{0:T(1024)(128)(4,1)S(1)} %broadcast_compare_fusion.2, bf16[2,512,512]{2,1,0:T(8,128)(2,1)} %get-tuple-element.126, s32[]{:T(128)} %get-tuple-element.114), kind=kOutput, calls=%fused_computation.5.clone.1 | convolution fusion | flops 8623489024 | bytes 17322496 | tf_op jit(solution)/shard_map/while/body/eval_jaxpr/rd,cd->rc/dot_general | solution.py:29
  143.9 14.8 %select_reduce_fusion.2 = f32[512]{0:T(512)S(1)} fusion(bf16[16384,512]{1,0:T(8,128)(2,1)} %get-tuple-element.127, s32[512]{0:T(512)S(1)} %bitcast.35, pred[16384]{0:T(1024)(128)(4,1)S(1)} %broadcast_compare_fusion.2, bf16[2,512,512]{2,1,0:T(8,128)(2,1)} %get-tuple-element.126, s32[]{:T(128)} %get-tuple-element.114), kind=kOutput, calls=%fused_computation.5.clone.1 | convolution fusion | flops 8623489024 | bytes 17322496 | tf_op jit(solution)/shard_map/while/body/eval_jaxpr/rd,cd->rc/dot_general | solution.py:29
  158.8 0.6 all_to_all.18
  159.4 6.3 %all-to-all-start.2 = ((f32[8,1,128]{2,1,0:T(1,128)}), f32[8,1,128]{2,1,0:T(1,128)S(1)}, u32[]{:S(2)}, u32[]{:S(2)}) async-start(f32[8,1,128]{2,1,0:T(1,128)} %all_to_all.18), calls=%async_computation.2 | async-start | bytes 8192 | tf_op jit(solution)/shard_map/all_to_all | solution.py:78
  165.7 6.5 %all-to-all-done.2 = f32[8,1,128]{2,1,0:T(1,128)S(1)} async-done(((f32[8,1,128]{2,1,0:T(1,128)}), f32[8,1,128]{2,1,0:T(1,128)S(1)}, u32[]{:S(2)}, u32[]{:S(2)}) %all-to-all-start.2) | async-done | bytes 4128 | tf_op jit(solution)/shard_map/all_to_all | solution.py:78
  172.2 3.0 %gather_fusion = f32[384]{0:T(512)} fusion(f32[1024]{0:T(1024)S(1)} %bitcast.30, s32[1024]{0:T(1024)S(1)} %pad_clamp_fusion), kind=kCustom, calls=%fused_computation | custom fusion | bytes 4608 | tf_op jit(solution)/shard_map/gather | solution.py:81
  (14 shorter events, 0.2 us)
Async XLA Ops:
  6.5 122.4 %all-gather.2.cloned.1.call-start = ((), (), s32[]{:S(2)}) async-start(), calls=%async_computation.3 | async-start | bytes 17825792 | tf_op jit(solution)/shard_map/all_gather | solution.py:74
  40.3 9.9 %all-to-all-start = ((bf16[8,1,128]{2,1,0:T(2,128)(2,1)}), bf16[8,1,128]{2,1,0:T(2,128)(2,1)S(1)}, u32[]{:S(2)}, u32[]{:S(2)}) async-start(bf16[8,1,128]{2,1,0:T(2,128)(2,1)} %copy.3), calls=%async_computation | async-start | bytes 8192 | tf_op jit(solution)/shard_map/all_to_all | solution.py:65
  159.4 12.8 %all-to-all-start.2 = ((f32[8,1,128]{2,1,0:T(1,128)}), f32[8,1,128]{2,1,0:T(1,128)S(1)}, u32[]{:S(2)}, u32[]{:S(2)}) async-start(f32[8,1,128]{2,1,0:T(1,128)} %all_to_all.18), calls=%async_computation.2 | async-start | bytes 8192 | tf_op jit(solution)/shard_map/all_to_all | solution.py:78
Sparse Core Ops, SparseCore 0:
  36.8 92.1 all-gather.1
where the time goes:
time: 182 us
  waiting for transfers between devices  58.4 us (32%)
  blocking collectives  56.7 us (31%)
  matrix products  29.6 us (16%)
  between operations  13.4 us (7%)
  starting transfers between devices  9.88 us (5%)
  local copies, waits for them, and re-layouts  7.48 us (4%)
  other arithmetic  6.48 us (4%)
    all_gather x1, waiting for transfers between devices, local(): column_data = lax.all_gather(members, ('col', 'blk'), axis=0, tiled=True)  45.6 us
    all_gather x1, blocking collectives, local(): lax.all_gather(occupied, ('col', 'blk'), axis=0, tiled=True)  33.2 us
    dot_general x2, matrix products, one_block(): jnp.einsum('rd,cd->rc', row_piece, column_data, preferred_element_type=jn...  29.6 us
    all_to_all x1, blocking collectives, local(): lax.all_to_all(buffer.reshape(groups, CAP, features), 'cluster', split_ax...  23.5 us
    all_to_all x1, waiting for transfers between devices, local(): lax.all_to_all(own_best.reshape(groups, CAP), 'cluster', split_axis=0, co...  6.49 us
    all_to_all x1, waiting for transfers between devices, local(): lax.all_to_all(filled.reshape(groups, CAP), 'cluster', split_axis=0, conc...  6.34 us
    all_to_all x1, starting transfers between devices, local(): lax.all_to_all(own_best.reshape(groups, CAP), 'cluster', split_axis=0, co...  6.29 us
  transfers between devices with their start and end apart: 3, of which 3 were waited for; matrix products, arithmetic and copies ran while one was open for 2% of the time, Pallas kernels for 0%

commit v1 on v0

v1 whole, which is shorter than its diff:
```python
import jax
import jax.numpy as jnp
from jax import lax
from jax.experimental import pallas as pl
from jax.experimental.pallas import tpu as pltpu
from jax.sharding import PartitionSpec as P

MESH = pl.DeviceIdType.MESH
NT = (((1,), (1,)), ((), ()))
NEG = float("-inf")
PIECES = 3
PIECE = 128
DIRECTIONS = [(1, 0, 0), (-1, 0, 0), (0, 1, 0), (0, -1, 0), (0, 0, 1), (0, 0, -1)]
TWIST = 1
SLOTS = [
    (0, 0, 0), (0, 0, 1), (0, 0, 3), (0, 1, 0), (0, 1, 1), (0, 2, 0), (0, 2, 1), (1, 0, 3), (2, 0, 0), (2, 0, 3),
    (3, 0, 0), (3, 0, 3), (3, 3, 0),
]
SENDS = [
    (0, 1, 1, 5), (0, 2, 0, 4), (0, 3, 1, 3), (0, 10, 1, 0), (0, 2, 1, 4), (0, 10, 0, 0), (0, 1, 2, 5), (0, 3, 2,
    3), (10, 12, 1, 2), (2, 7, 0, 1), (3, 5, 1, 3), (3, 11, 1, 4), (2, 11, 0, 0), (10, 4, 1, 5), (10, 12, 0, 2), (2,
    7, 1, 1), (10, 8, 0, 0), (10, 4, 0, 5), (3, 11, 2, 4), (3, 5, 2, 3), (7, 9, 0, 1), (11, 3, 0, 5), (0, 2, 2, 4),
    (0, 10, 2, 0), (1, 4, 2, 3), (7, 9, 1, 1), (4, 1, 0, 2), (8, 6, 0, 5), (5, 9, 2, 4), (10, 8, 1, 0), (4, 6, 1,
    3), (10, 12, 2, 2), (2, 7, 2, 1), (10, 8, 2, 0), (9, 5, 0, 5), (4, 6, 2, 3),
]
STEPS = [
    (0, 0, []),
    (0, 1, []),
    (0, 2, []),
    (1, 1, [(0, 0), (0, 1), (0, 2)]),
    (2, 0, [(0, 0), (0, 2), (1, 1)]),
    (3, 1, [(0, 0), (0, 1), (0, 2), (1, 1), (2, 0)]),
    (10, 1, [(0, 0), (0, 1), (0, 2), (1, 1), (2, 0), (3, 1)]),
    (1, 2, [(0, 1), (0, 2), (2, 0), (3, 1), (10, 1)]),
    (2, 1, [(0, 0), (1, 1), (1, 2), (3, 1), (10, 1)]),
    (3, 2, [(0, 0), (0, 1), (0, 2), (1, 1), (1, 2), (2, 0), (2, 1), (10, 1)]),
    (10, 0, [(0, 0), (0, 1), (0, 2), (1, 1), (1, 2), (2, 0), (2, 1), (3, 1), (3, 2)]),
    (7, 0, [(0, 2), (1, 1), (1, 2), (2, 0), (3, 1), (3, 2), (10, 0), (10, 1)]),
    (12, 1, [(0, 0), (1, 1), (1, 2), (2, 0), (3, 1), (3, 2), (7, 0), (10, 0)]),
    (4, 1, [(0, 2), (2, 0), (2, 1), (7, 0), (12, 1)]),
    (5, 1, [(0, 0), (0, 1), (0, 2), (1, 1), (1, 2), (2, 0), (2, 1), (7, 0), (10, 0), (12, 1)]),
    (11, 0, [(0, 0), (0, 1), (0, 2), (1, 1), (1, 2), (3, 1), (3, 2), (4, 1), (5, 1), (7, 0)]),
    (11, 1, [(0, 0), (1, 1), (1, 2), (3, 1), (3, 2), (4, 1), (5, 1)]),
    (7, 1, [(0, 2), (1, 2), (3, 1), (3, 2), (4, 1), (5, 1), (10, 0)]),
    (12, 0, [(0, 0), (1, 2), (2, 0), (2, 1), (3, 2), (5, 1), (7, 0), (7, 1), (11, 0), (11, 1)]),
    (4, 0, [(0, 2), (2, 0), (2, 1), (3, 2), (7, 0), (7, 1), (11, 0), (11, 1)]),
    (5, 2, [(0, 0), (0, 2), (1, 1), (1, 2), (2, 0), (2, 1), (4, 0), (7, 0), (7, 1), (11, 0), (11, 1), (12, 0), (12, 1)]),
    (8, 0, [(0, 0), (0, 1), (0, 2), (3, 1), (3, 2), (4, 0), (5, 1), (5, 2), (12, 0)]),
    (11, 2, [(1, 2), (3, 1), (3, 2), (4, 0), (4, 1), (5, 1), (5, 2), (12, 0), (12, 1)]),
    (9, 0, [(0, 2), (1, 1), (1, 2), (3, 1), (3, 2), (4, 0), (4, 1), (5, 1), (5, 2), (11, 2), (12, 0), (12, 1)]),
    (2, 2, [(1, 2), (3, 1), (3, 2), (4, 0), (4, 1), (5, 1), (5, 2), (8, 0), (12, 0), (12, 1)]),
    (3, 0, [(2, 0), (2, 1), (2, 2), (7, 0), (7, 1), (8, 0), (9, 0), (11, 0), (11, 1), (11, 2), (12, 0), (12, 1)]),
    (4, 2, [(0, 2), (1, 1), (1, 2), (2, 0), (2, 1), (2, 2), (7, 0), (7, 1), (9, 0), (11, 0), (11, 1), (11, 2), (12, 0), (12, 1)]),
    (10, 2, [(0, 0), (1, 2), (3, 0), (3, 1), (3, 2), (4, 2), (5, 1), (5, 2)]),
    (1, 0, [(2, 0), (7, 0), (8, 0), (9, 0)]),
    (9, 1, [(1, 1), (1, 2), (3, 0), (3, 1), (3, 2), (4, 0), (4, 1), (4, 2), (5, 1), (5, 2), (12, 0), (12, 1)]),
    (6, 0, [(2, 0), (2, 1), (2, 2), (7, 0), (7, 1), (8, 0), (9, 0), (9, 1), (10, 2), (11, 1), (11, 2)]),
    (6, 1, [(1, 1), (1, 2), (2, 1), (2, 2), (9, 1), (10, 2), (11, 1), (11, 2)]),
    (8, 1, [(1, 0), (3, 0), (3, 1), (3, 2), (4, 0), (5, 1), (5, 2), (6, 0), (12, 0)]),
    (9, 2, [(1, 2), (3, 0), (3, 1), (3, 2), (4, 0), (4, 1), (4, 2), (5, 1), (5, 2), (6, 0), (6, 1), (12, 0), (12, 1)]),
    (7, 2, [(3, 0), (3, 1), (3, 2), (4, 0), (4, 1), (4, 2), (5, 1), (5, 2), (6, 0), (6, 1)]),
    (12, 2, [(3, 0), (4, 2), (5, 1), (5, 2), (9, 0), (9, 1), (9, 2)]),
    (5, 0, [(2, 2), (7, 2), (8, 0), (9, 2), (11, 0), (11, 1), (11, 2), (12, 2)]),
    (6, 2, [(1, 2), (2, 2), (9, 2), (11, 2)]),
    (8, 2, [(3, 0), (3, 1), (3, 2), (5, 2)]),
]
ORDER = [
    (1, 0), (1, 1), (1, 2), (1, 3), (2, 0), (2, 1), (2, 2), (1, 4), (1, 5), (1, 6), (1, 7), (0, 0), (0, 1), (0, 2),
    (0, 3), (1, 8), (1, 9), (1, 10), (1, 11), (1, 12), (1, 13), (2, 3), (2, 4), (2, 5), (2, 6), (0, 4), (0, 5), (0,
    6), (0, 7), (1, 14), (1, 15), (1, 16), (1, 17), (1, 18), (1, 19), (2, 7), (2, 8), (2, 9), (2, 10), (0, 8), (0,
    9), (1, 20), (0, 10), (0, 11), (0, 12), (0, 13), (2, 11), (1, 21), (1, 22), (1, 23), (1, 24), (2, 12), (2, 13),
    (2, 14), (2, 15), (0, 14), (0, 15), (2, 16), (0, 16), (0, 17), (0, 18), (0, 19), (1, 25), (1, 26), (2, 17), (1,
    27), (1, 28), (1, 29), (1, 30), (2, 18), (2, 19), (2, 20), (2, 21), (0, 20), (2, 22), (0, 21), (0, 22), (0, 23),
    (0, 24), (1, 31), (1, 32), (2, 23), (1, 33), (1, 34), (1, 35), (2, 24), (2, 25), (2, 26), (0, 25), (0, 26), (2,
    27), (3, 0), (0, 27), (0, 28), (0, 29), (0, 30), (2, 28), (2, 29), (2, 30), (2, 31), (3, 10), (2, 32), (0, 31),
    (0, 32), (2, 33), (0, 33), (0, 34), (0, 35), (2, 34), (2, 35), (3, 4), (2, 36), (3, 7), (3, 12), (2, 37), (3,
    1), (3, 2), (3, 11), (3, 9), (3, 6), (2, 38), (3, 3), (3, 5), (3, 8),
]


def device_at(offset, core):
    cluster = lax.axis_index("cluster")
    blk = lax.axis_index("blk")
    x, y, z = blk % 4, cluster // 2, (cluster % 2) * 2 + blk // 4
    odd = z % 2
    dx, dy, dz = offset
    if TWIST == 1:
        dx, dy = dx - odd * (dx + dy), dy - odd * (dx + dy)
    elif TWIST == 2:
        dx, dy = dx + odd * (dy - dx), dy + odd * (dx - dy)
    elif TWIST == 3:
        dx, dy = dx - odd * (2 * dx), dy - odd * (2 * dy)
    elif TWIST == 4:
        dx = dx - odd * (2 * dx)
    x, y, z = (x + dx + 8) % 4, (y + dy + 8) % 4, (z + dz + 8) % 4
    return (y * 2 + z // 2, core, (z % 2) * 4 + x)


def kernel(
    x_ref, id_ref, o_ref, x_in, id_in, rows, ids, id_rows, row_best, col_best, partial, returned,
    load_sem, send_sem, recv_sem, id_send, id_recv, twin_send, twin_recv, twin_id_send, twin_id_recv,
    home_send, home_recv,
):
    core = lax.axis_index("col")
    twin = 1 - core
    here = (0, 0, 0)
    slots = len(SLOTS)

    barrier = pltpu.get_barrier_semaphore()
    for direction in DIRECTIONS:
        pl.semaphore_signal(barrier, inc=1, device_id=device_at(direction, core), device_id_type=MESH)
    pl.semaphore_signal(barrier, inc=1, device_id=device_at(here, twin), device_id_type=MESH)
    load = pltpu.make_async_copy(x_ref, x_in, load_sem.at[0])
    load_ids = pltpu.make_async_copy(id_ref, id_in, load_sem.at[1])
    load.start()
    load_ids.start()

    def remote(src, dst, send, recv, device):
        return pltpu.make_async_remote_copy(
            src_ref=src, dst_ref=dst, send_sem=send, recv_sem=recv, device_id=device, device_id_type=MESH
        )

    def spread_ids(slot):
        for piece in range(PIECES):
            lane_ids = ids[slot, core, :, piece * PIECE:(piece + 1) * PIECE]
            id_rows[slot, piece] = jnp.broadcast_to(lane_ids, (PIECE, PIECE)).T

    started = []

    def start(copy):
        copy.start()
        started.append(copy)

    def to_twin(slot, piece):
        copy = remote(
            rows.at[slot, piece, core], rows.at[slot, piece, core],
            twin_send.at[slot, piece], twin_recv.at[slot, piece], device_at(here, twin),
        )
        start(copy)

    def ids_to_twin(slot):
        copy = remote(
            ids.at[slot, core], ids.at[slot, core], twin_id_send.at[slot], twin_id_recv.at[slot],
            device_at(here, twin),
        )
        start(copy)

    def twin_wait(slot, piece):
        remote(
            rows.at[slot, piece, twin], rows.at[slot, piece, twin],
            twin_send.at[slot, piece], twin_recv.at[slot, piece], device_at(here, twin),
        ).wait_recv()

    def twin_ids_wait(slot):
        remote(
            ids.at[slot, twin], ids.at[slot, twin], twin_id_send.at[slot], twin_id_recv.at[slot],
            device_at(here, twin),
        ).wait_recv()

    load_ids.wait()
    ids[0, core] = id_in[...].astype(jnp.float32)
    load.wait()
    features = x_in.shape[1]
    for piece in range(PIECES):
        values = x_in[piece * PIECE:(piece + 1) * PIECE].astype(jnp.float32)
        mean = jnp.mean(values * values, axis=-1, keepdims=True)
        scale = lax.rsqrt(mean + 1e-06) * (1.0 / features**0.5)
        rows[0, piece, core] = (values * scale).astype(jnp.bfloat16)
    pl.semaphore_wait(barrier, len(DIRECTIONS) + 1)

    id_fresh, twin_id_fresh = set(), set()
    row_touched, col_touched = set(), set()

    def piece_copy(index):
        src, dst, piece, direction = SENDS[index]
        return remote(
            rows.at[src, piece, core], rows.at[dst, piece, core],
            send_sem.at[index], recv_sem.at[dst, piece], device_at(DIRECTIONS[direction], core),
        )

    def id_copy(index):
        src, dst, piece, direction = SENDS[index]
        return remote(
            ids.at[src, core], ids.at[dst, core], id_send.at[dst], id_recv.at[dst],
            device_at(DIRECTIONS[direction], core),
        )

    first_for = {}
    for index, (src, dst, piece, direction) in enumerate(SENDS):
        first_for.setdefault(dst, index)

    def arrive(index):
        src, dst, piece, direction = SENDS[index]
        if first_for[dst] == index:
            id_copy(index).wait_recv()
            ids_to_twin(dst)
        piece_copy(index).wait_recv()
        to_twin(dst, piece)
        if first_for[dst] == index:
            spread_ids(dst)

    def send(index):
        src, dst, piece, direction = SENDS[index]
        start(piece_copy(index))
        if first_for[dst] == index:
            start(id_copy(index))

    def step(index):
        slot, piece, others = STEPS[index]
        if slot not in twin_id_fresh:
            twin_id_fresh.add(slot)
            twin_ids_wait(slot)
        twin_wait(slot, piece)
        own = [(0, p) for p in range(PIECES)] if slot == 0 else []
        left = others + own
        columns = rows[slot, piece].reshape(2 * PIECE, features)
        stacked = jnp.concatenate([rows[s, p, core] for s, p in left], axis=0)
        scores = lax.dot_general(stacked, columns, NT, preferred_element_type=jnp.float32)
        for half in range(2):
            lane_ids = ids[slot, half, :, piece * PIECE:(piece + 1) * PIECE]
            columns_best = None
            for at, (s, p) in enumerate(left):
                block = scores[at * PIECE:(at + 1) * PIECE, half * PIECE:(half + 1) * PIECE]
                allowed = id_rows[s, p] == lane_ids
                if (s, p) in own and p == piece:
                    r = lax.broadcasted_iota(jnp.int32, (PIECE, PIECE), 0)
                    c = lax.broadcasted_iota(jnp.int32, (PIECE, PIECE), 1)
                    allowed = allowed & (r + PIECE * core != c + PIECE * half)
                block = jnp.where(allowed, block, NEG)
                if (s, p) in row_touched:
                    row_best[s, p] = jnp.maximum(row_best[s, p], block)
                else:
                    row_best[s, p] = block
                    row_touched.add((s, p))
                if slot != 0:
                    best = jnp.max(block.reshape(PIECE // 8, 8, PIECE), axis=0)
                    columns_best = best if columns_best is None else jnp.maximum(columns_best, best)
            if columns_best is not None:
                col_best[slot, piece, half] = columns_best
                col_touched.add((slot, piece))

    def home_copy(slot, to_core):
        if slot == 0:
            return remote(
                partial.at[0, twin], returned.at[0, core], home_send.at[0, 0], home_recv.at[0, core],
                device_at(here, twin),
            )
        return remote(
            partial.at[slot, to_core], returned.at[slot, core], home_send.at[slot, to_core],
            home_recv.at[slot, core], device_at(SLOTS[slot], to_core),
        )

    def go_home(slot):
        for piece in range(PIECES):
            mine = None
            if (slot, piece) in row_touched:
                mine = jnp.max(row_best[slot, piece].T, axis=0, keepdims=True)
            for half in range(2):
                best = jnp.full((1, PIECE), NEG, jnp.float32)
                if mine is not None:
                    best = jnp.where(core == half, mine, best)
                if (slot, piece) in col_touched:
                    best = jnp.maximum(best, jnp.max(col_best[slot, piece, half], axis=0, keepdims=True))
                partial[slot, half, :, piece * PIECE:(piece + 1) * PIECE] = best
        if slot == 0:
            start(home_copy(0, None))
        else:
            for to_core in range(2):
                start(home_copy(slot, to_core))

    for piece in range(PIECES):
        to_twin(0, piece)
    ids_to_twin(0)
    spread = False
    for kind, index in ORDER:
        if kind == 2 and not spread:
            spread = True
            spread_ids(0)
        (arrive, send, step, go_home)[kind](index)

    best = partial[0, core]
    remote(
        partial.at[0, core], returned.at[0, twin], home_send.at[0, 0], home_recv.at[0, twin], device_at(here, twin)
    ).wait_recv()
    best = jnp.maximum(best, returned[0, twin])
    for slot in range(1, slots):
        for half in range(2):
            remote(
                partial.at[slot, half], returned.at[slot, half], home_send.at[slot, half],
                home_recv.at[slot, half], device_at(here, twin),
            ).wait_recv()
            best = jnp.maximum(best, returned[slot, half])
    o_ref[...] = best
    for copy in started:
        copy.wait_send()


def local(embeddings, assignment):
    count, features = embeddings.shape
    slots = len(SLOTS)
    dma = pltpu.SemaphoreType.DMA
    best = pl.pallas_call(
        kernel,
        out_shape=jax.ShapeDtypeStruct((1, count), jnp.float32),
        in_specs=[pl.BlockSpec(memory_space=pl.ANY)] * 2,
        out_specs=pl.BlockSpec(memory_space=pltpu.VMEM),
        scratch_shapes=[
            pltpu.VMEM((count, features), jnp.bfloat16),
            pltpu.VMEM((1, count), jnp.int32),
            pltpu.VMEM((slots, PIECES, 2, PIECE, features), jnp.bfloat16),
            pltpu.VMEM((slots, 2, 1, count), jnp.float32),
            pltpu.VMEM((slots, PIECES, PIECE, PIECE), jnp.float32),
            pltpu.VMEM((slots, PIECES, PIECE, PIECE), jnp.float32),
            pltpu.VMEM((slots, PIECES, 2, 8, PIECE), jnp.float32),
            pltpu.VMEM((slots, 2, 1, count), jnp.float32),
            pltpu.VMEM((slots, 2, 1, count), jnp.float32),
            dma((2,)),
            dma((len(SENDS),)),
            dma((slots, PIECES)),
            dma((slots,)),
            dma((slots,)),
            dma((slots, PIECES)),
            dma((slots, PIECES)),
            dma((slots,)),
            dma((slots,)),
            dma((slots, 2)),
            dma((slots, 2)),
        ],
        compiler_params=pltpu.CompilerParams(
            collective_id=0, has_side_effects=True, vmem_limit_bytes=56 * 2**20
        ),
    )(embeddings, assignment.reshape(1, count))
    return best.reshape(count)


def solution(mesh):
    axes = ("cluster", "col", "blk")
    return jax.shard_map(
        local, mesh=mesh, in_specs=(P(axes, None), P(axes, None)), out_specs=P(axes), check_vma=False
    )
```

time: 182 us -> 53.5 us (0.29)
  waiting for transfers between devices: 58.4 us -> 0 us
  blocking collectives: 56.7 us -> 0 us
  Pallas kernels: 0 us -> 52.1 us
  matrix products: 29.6 us -> 0 us
  between operations: 13.4 us -> 0.01 us
  starting transfers between devices: 9.88 us -> 0 us
  local copies, waits for them, and re-layouts: 7.48 us -> 0 us
  other arithmetic: 6.48 us -> 1.28 us
    pallas_call x0 -> x1, Pallas kernels: none -> 52.1 us  [local(): pl.pallas_call(kernel, out_shape=jax.ShapeDtypeStruct((1, count), jnp.flo...]
    all_gather x1 -> x0, waiting for transfers between devices: 45.6 us -> none  [local(): column_data = lax.all_gather(members, ('col', 'blk'), axis=0, tiled=True)]
    all_gather x1 -> x0, blocking collectives: 33.2 us -> none  [local(): lax.all_gather(occupied, ('col', 'blk'), axis=0, tiled=True)]
    dot_general x2 -> x0, matrix products: 29.6 us -> none  [one_block(): jnp.einsum('rd,cd->rc', row_piece, column_data, preferred_element_type=jn...]
    all_to_all x1 -> x0, blocking collectives: 23.5 us -> none  [local(): lax.all_to_all(buffer.reshape(groups, CAP, features), 'cluster', split_ax...]
    all_to_all x2 -> x0, waiting for transfers between devices: 12.8 us -> none  [the longest x1 6.49 us: local(): lax.all_to_all(own_best.reshape(groups, CAP), 'cluster', split_axis=0, co...]
    all_to_all x2 -> x0, starting transfers between devices: 9.88 us -> none  [the longest x1 6.29 us: local(): lax.all_to_all(own_best.reshape(groups, CAP), 'cluster', split_axis=0, co...]
    gather x1 -> x0, local copies, waits for them, and re-layouts: 3 us -> none  [local(): return returned.reshape(slots)[target]]
  transfers between devices with their start and end apart: 3 -> 0, of which waited for: 3 -> 0; matrix products, arithmetic and copies ran while one was open for 2% -> 0% of each run, Pallas kernels for 0% -> 0%
where the time goes in v1:
time: 53.5 us; the launch traced here: 53.3 us
  Pallas kernels  52.1 us (97%)
  other arithmetic  1.28 us (2%)
    pallas_call x1, Pallas kernels, local(): pl.pallas_call(kernel, out_shape=jax.ShapeDtypeStruct((1, count), jnp.flo...  52.1 us
    pallas_call x1, other arithmetic, local(): pl.pallas_call(kernel, out_shape=jax.ShapeDtypeStruct((1, count), jnp.flo...  1.28 us

profile of v1, /device:TPU:1, one launch (start us, length us, event | category | flops | bytes accessed | tf_op | source)
XLA Modules:
  0.0 53.3 jit_solution(15252594896433379868)
XLA Ops:
  0.0 52.1 %shard_map.28 = f32[1,384]{1,0:T(1,128)} custom-call(bf16[384,512]{1,0:T(8,128)(2,1)} %x_ref.1, s32[1,384]{1,0:T(1,128)} %bitcast.1), custom_call_target="tpu_custom_call" | custom-call | tf_op jit(solution)/shard_map/pallas_call | solution.py:302
  52.1 1.3 %reduce = f32[384]{0:T(512)} reduce(f32[1,384]{1,0:T(1,128)} %shard_map.28, f32[]{:T(128)} %constant), dimensions={0}, to_apply=%pallas_call.3.reduce_sub_computation | reduce | bytes 3076 | tf_op jit(solution)/shard_map/pallas_call | solution.py:302

commit v2 on v1

--- a/solution.py
+++ b/solution.py
@@ -11,70 +11,70 @@
 PIECES = 3
 PIECE = 128
 DIRECTIONS = [(1, 0, 0), (-1, 0, 0), (0, 1, 0), (0, -1, 0), (0, 0, 1), (0, 0, -1)]
-TWIST = 1
+TWIST = 4
 SLOTS = [
-    (0, 0, 0), (0, 0, 1), (0, 0, 3), (0, 1, 0), (0, 1, 1), (0, 2, 0), (0, 2, 1), (1, 0, 3), (2, 0, 0), (2, 0, 3),
-    (3, 0, 0), (3, 0, 3), (3, 3, 0),
+    (0, 0, 0), (0, 0, 1), (0, 0, 3), (0, 1, 0), (0, 1, 3), (0, 2, 0), (0, 2, 3), (0, 3, 0), (1, 0, 0), (1, 0, 1),
+    (2, 0, 0), (2, 0, 1), (3, 0, 1), (3, 0, 2),
 ]
 SENDS = [
-    (0, 1, 1, 5), (0, 2, 0, 4), (0, 3, 1, 3), (0, 10, 1, 0), (0, 2, 1, 4), (0, 10, 0, 0), (0, 1, 2, 5), (0, 3, 2,
-    3), (10, 12, 1, 2), (2, 7, 0, 1), (3, 5, 1, 3), (3, 11, 1, 4), (2, 11, 0, 0), (10, 4, 1, 5), (10, 12, 0, 2), (2,
-    7, 1, 1), (10, 8, 0, 0), (10, 4, 0, 5), (3, 11, 2, 4), (3, 5, 2, 3), (7, 9, 0, 1), (11, 3, 0, 5), (0, 2, 2, 4),
-    (0, 10, 2, 0), (1, 4, 2, 3), (7, 9, 1, 1), (4, 1, 0, 2), (8, 6, 0, 5), (5, 9, 2, 4), (10, 8, 1, 0), (4, 6, 1,
-    3), (10, 12, 2, 2), (2, 7, 2, 1), (10, 8, 2, 0), (9, 5, 0, 5), (4, 6, 2, 3),
+    (0, 8, 1, 1), (0, 7, 2, 2), (0, 3, 1, 3), (0, 2, 2, 4), (0, 1, 0, 5), (0, 8, 0, 1), (0, 7, 0, 2), (0, 3, 0, 3),
+    (0, 2, 0, 4), (0, 1, 2, 5), (0, 8, 2, 1), (0, 7, 1, 2), (0, 3, 2, 3), (0, 2, 1, 4), (0, 1, 1, 5), (1, 12, 0, 0),
+    (8, 10, 1, 1), (7, 5, 2, 2), (2, 4, 2, 3), (3, 4, 1, 4), (8, 12, 1, 5), (1, 12, 2, 0), (1, 9, 2, 1), (7, 5, 0,
+    2), (2, 4, 0, 3), (12, 11, 0, 0), (8, 10, 0, 1), (7, 5, 1, 2), (10, 11, 1, 5), (5, 6, 2, 4), (4, 6, 1, 3), (8,
+    10, 2, 1), (12, 11, 2, 0), (9, 13, 2, 5), (5, 6, 0, 4), (11, 9, 0, 0), (1, 9, 1, 1),
 ]
 STEPS = [
     (0, 0, []),
     (0, 1, []),
     (0, 2, []),
-    (1, 1, [(0, 0), (0, 1), (0, 2)]),
-    (2, 0, [(0, 0), (0, 2), (1, 1)]),
-    (3, 1, [(0, 0), (0, 1), (0, 2), (1, 1), (2, 0)]),
-    (10, 1, [(0, 0), (0, 1), (0, 2), (1, 1), (2, 0), (3, 1)]),
-    (1, 2, [(0, 1), (0, 2), (2, 0), (3, 1), (10, 1)]),
-    (2, 1, [(0, 0), (1, 1), (1, 2), (3, 1), (10, 1)]),
-    (3, 2, [(0, 0), (0, 1), (0, 2), (1, 1), (1, 2), (2, 0), (2, 1), (10, 1)]),
-    (10, 0, [(0, 0), (0, 1), (0, 2), (1, 1), (1, 2), (2, 0), (2, 1), (3, 1), (3, 2)]),
-    (7, 0, [(0, 2), (1, 1), (1, 2), (2, 0), (3, 1), (3, 2), (10, 0), (10, 1)]),
-    (12, 1, [(0, 0), (1, 1), (1, 2), (2, 0), (3, 1), (3, 2), (7, 0), (10, 0)]),
-    (4, 1, [(0, 2), (2, 0), (2, 1), (7, 0), (12, 1)]),
-    (5, 1, [(0, 0), (0, 1), (0, 2), (1, 1), (1, 2), (2, 0), (2, 1), (7, 0), (10, 0), (12, 1)]),
-    (11, 0, [(0, 0), (0, 1), (0, 2), (1, 1), (1, 2), (3, 1), (3, 2), (4, 1), (5, 1), (7, 0)]),
-    (11, 1, [(0, 0), (1, 1), (1, 2), (3, 1), (3, 2), (4, 1), (5, 1)]),
-    (7, 1, [(0, 2), (1, 2), (3, 1), (3, 2), (4, 1), (5, 1), (10, 0)]),
-    (12, 0, [(0, 0), (1, 2), (2, 0), (2, 1), (3, 2), (5, 1), (7, 0), (7, 1), (11, 0), (11, 1)]),
-    (4, 0, [(0, 2), (2, 0), (2, 1), (3, 2), (7, 0), (7, 1), (11, 0), (11, 1)]),
-    (5, 2, [(0, 0), (0, 2), (1, 1), (1, 2), (2, 0), (2, 1), (4, 0), (7, 0), (7, 1), (11, 0), (11, 1), (12, 0), (12, 1)]),
-    (8, 0, [(0, 0), (0, 1), (0, 2), (3, 1), (3, 2), (4, 0), (5, 1), (5, 2), (12, 0)]),
-    (11, 2, [(1, 2), (3, 1), (3, 2), (4, 0), (4, 1), (5, 1), (5, 2), (12, 0), (12, 1)]),
-    (9, 0, [(0, 2), (1, 1), (1, 2), (3, 1), (3, 2), (4, 0), (4, 1), (5, 1), (5, 2), (11, 2), (12, 0), (12, 1)]),
-    (2, 2, [(1, 2), (3, 1), (3, 2), (4, 0), (4, 1), (5, 1), (5, 2), (8, 0), (12, 0), (12, 1)]),
-    (3, 0, [(2, 0), (2, 1), (2, 2), (7, 0), (7, 1), (8, 0), (9, 0), (11, 0), (11, 1), (11, 2), (12, 0), (12, 1)]),
-    (4, 2, [(0, 2), (1, 1), (1, 2), (2, 0), (2, 1), (2, 2), (7, 0), (7, 1), (9, 0), (11, 0), (11, 1), (11, 2), (12, 0), (12, 1)]),
-    (10, 2, [(0, 0), (1, 2), (3, 0), (3, 1), (3, 2), (4, 2), (5, 1), (5, 2)]),
-    (1, 0, [(2, 0), (7, 0), (8, 0), (9, 0)]),
-    (9, 1, [(1, 1), (1, 2), (3, 0), (3, 1), (3, 2), (4, 0), (4, 1), (4, 2), (5, 1), (5, 2), (12, 0), (12, 1)]),
-    (6, 0, [(2, 0), (2, 1), (2, 2), (7, 0), (7, 1), (8, 0), (9, 0), (9, 1), (10, 2), (11, 1), (11, 2)]),
-    (6, 1, [(1, 1), (1, 2), (2, 1), (2, 2), (9, 1), (10, 2), (11, 1), (11, 2)]),
-    (8, 1, [(1, 0), (3, 0), (3, 1), (3, 2), (4, 0), (5, 1), (5, 2), (6, 0), (12, 0)]),
-    (9, 2, [(1, 2), (3, 0), (3, 1), (3, 2), (4, 0), (4, 1), (4, 2), (5, 1), (5, 2), (6, 0), (6, 1), (12, 0), (12, 1)]),
-    (7, 2, [(3, 0), (3, 1), (3, 2), (4, 0), (4, 1), (4, 2), (5, 1), (5, 2), (6, 0), (6, 1)]),
-    (12, 2, [(3, 0), (4, 2), (5, 1), (5, 2), (9, 0), (9, 1), (9, 2)]),
-    (5, 0, [(2, 2), (7, 2), (8, 0), (9, 2), (11, 0), (11, 1), (11, 2), (12, 2)]),
-    (6, 2, [(1, 2), (2, 2), (9, 2), (11, 2)]),
-    (8, 2, [(3, 0), (3, 1), (3, 2), (5, 2)]),
+    (8, 1, [(0, 0), (0, 1), (0, 2), (1, 0), (2, 2), (3, 1), (7, 2)]),
+    (7, 2, [(0, 0), (0, 1), (0, 2), (1, 0), (2, 2), (3, 1)]),
+    (2, 2, [(0, 0), (0, 1), (0, 2), (1, 0), (3, 1)]),
+    (3, 1, [(0, 0), (0, 1), (1, 0)]),
+    (1, 0, [(0, 0), (0, 1)]),
+    (8, 0, [(0, 0), (0, 1), (0, 2), (1, 0), (1, 2), (2, 2), (3, 0), (3, 1), (7, 0), (7, 2)]),
+    (7, 0, [(0, 0), (0, 2), (1, 0), (1, 2), (2, 0), (2, 2), (3, 0), (3, 1), (8, 1)]),
+    (1, 2, [(0, 0), (0, 1), (2, 2), (3, 0), (3, 1), (7, 2), (8, 1)]),
+    (2, 0, [(0, 1), (1, 0), (3, 1), (8, 1)]),
+    (3, 0, [(0, 1), (1, 1), (2, 1), (7, 2), (8, 1), (8, 2), (12, 0)]),
+    (8, 2, [(0, 0), (0, 1), (0, 2), (1, 2), (3, 1), (3, 2), (7, 0), (7, 1), (7, 2), (12, 0)]),
+    (7, 1, [(0, 2), (1, 1), (1, 2), (2, 1), (2, 2), (3, 1), (8, 0), (8, 1), (12, 0)]),
+    (12, 0, [(2, 0), (2, 1), (2, 2), (3, 1), (3, 2), (7, 0), (7, 2), (8, 0), (8, 1)]),
+    (2, 1, [(0, 1), (1, 0), (1, 1), (1, 2), (5, 2), (8, 1), (10, 1), (12, 1), (12, 2)]),
+    (3, 2, [(7, 2), (8, 0), (8, 1), (10, 1), (12, 1), (12, 2)]),
+    (1, 1, [(4, 1), (4, 2), (5, 2)]),
+    (10, 1, [(0, 0), (0, 1), (0, 2), (1, 2), (2, 0), (2, 2), (3, 0), (3, 1), (4, 1), (4, 2), (5, 2), (7, 0), (7, 2), (12, 0), (12, 1), (12, 2)]),
+    (5, 2, [(1, 0), (1, 2), (2, 0), (8, 0), (8, 1), (8, 2), (9, 2), (11, 0), (12, 0), (12, 1), (12, 2)]),
+    (12, 2, [(2, 0), (2, 2), (3, 0), (3, 1), (4, 0), (4, 1), (4, 2), (5, 0), (7, 0), (7, 1), (7, 2), (8, 0), (8, 2), (9, 2)]),
+    (12, 1, [(2, 0), (2, 2), (3, 0), (3, 1), (4, 0), (4, 1), (4, 2), (5, 0), (7, 0), (7, 1), (7, 2)]),
+    (4, 1, [(1, 0), (1, 2), (7, 0), (7, 1), (9, 2), (10, 0), (11, 0), (11, 1), (12, 0)]),
+    (4, 2, [(1, 0), (1, 2), (9, 2), (10, 0), (11, 0), (11, 1), (11, 2), (12, 0)]),
+    (9, 2, [(0, 0), (0, 2), (3, 0), (3, 1), (3, 2), (4, 0), (5, 0), (5, 1), (6, 1), (6, 2), (7, 0), (7, 1), (7, 2), (12, 0)]),
+    (11, 0, [(1, 0), (2, 0), (2, 1), (2, 2), (3, 0), (4, 0), (5, 0), (5, 1), (6, 1), (6, 2), (7, 0), (7, 1), (7, 2), (8, 0), (8, 2)]),
+    (5, 0, [(1, 0), (1, 1), (8, 0), (8, 1), (8, 2), (10, 0), (10, 1), (10, 2), (11, 1), (11, 2), (12, 0), (13, 2)]),
+    (4, 0, [(1, 0), (1, 1), (1, 2), (9, 0), (10, 1), (10, 2), (11, 1), (11, 2), (12, 0), (13, 2)]),
+    (6, 1, [(1, 0), (1, 1), (1, 2), (8, 0), (8, 1), (8, 2), (9, 0), (10, 1), (10, 2), (11, 1), (11, 2), (12, 0), (12, 1), (12, 2), (13, 2)]),
+    (11, 1, [(2, 1), (2, 2), (5, 2), (7, 0), (7, 1), (7, 2), (8, 0), (8, 2)]),
+    (5, 1, [(8, 0), (8, 1), (8, 2), (9, 0), (9, 1), (10, 1)]),
+    (10, 0, [(3, 0), (3, 2), (7, 2)]),
+    (6, 2, [(1, 0), (1, 2), (9, 0), (10, 2), (11, 2)]),
+    (11, 2, [(2, 2), (3, 1), (3, 2), (4, 1), (7, 0), (7, 1), (7, 2)]),
+    (6, 0, [(1, 0), (9, 0), (11, 0), (13, 2)]),
+    (10, 2, [(3, 2), (5, 2)]),
+    (9, 0, [(3, 0), (3, 1), (3, 2), (4, 1), (4, 2), (5, 0), (7, 0), (7, 1)]),
+    (9, 1, [(3, 0), (3, 1), (3, 2), (4, 0), (4, 1), (4, 2), (5, 0), (7, 0), (7, 1), (7, 2)]),
 ]
 ORDER = [
-    (1, 0), (1, 1), (1, 2), (1, 3), (2, 0), (2, 1), (2, 2), (1, 4), (1, 5), (1, 6), (1, 7), (0, 0), (0, 1), (0, 2),
-    (0, 3), (1, 8), (1, 9), (1, 10), (1, 11), (1, 12), (1, 13), (2, 3), (2, 4), (2, 5), (2, 6), (0, 4), (0, 5), (0,
-    6), (0, 7), (1, 14), (1, 15), (1, 16), (1, 17), (1, 18), (1, 19), (2, 7), (2, 8), (2, 9), (2, 10), (0, 8), (0,
-    9), (1, 20), (0, 10), (0, 11), (0, 12), (0, 13), (2, 11), (1, 21), (1, 22), (1, 23), (1, 24), (2, 12), (2, 13),
-    (2, 14), (2, 15), (0, 14), (0, 15), (2, 16), (0, 16), (0, 17), (0, 18), (0, 19), (1, 25), (1, 26), (2, 17), (1,
-    27), (1, 28), (1, 29), (1, 30), (2, 18), (2, 19), (2, 20), (2, 21), (0, 20), (2, 22), (0, 21), (0, 22), (0, 23),
-    (0, 24), (1, 31), (1, 32), (2, 23), (1, 33), (1, 34), (1, 35), (2, 24), (2, 25), (2, 26), (0, 25), (0, 26), (2,
-    27), (3, 0), (0, 27), (0, 28), (0, 29), (0, 30), (2, 28), (2, 29), (2, 30), (2, 31), (3, 10), (2, 32), (0, 31),
-    (0, 32), (2, 33), (0, 33), (0, 34), (0, 35), (2, 34), (2, 35), (3, 4), (2, 36), (3, 7), (3, 12), (2, 37), (3,
-    1), (3, 2), (3, 11), (3, 9), (3, 6), (2, 38), (3, 3), (3, 5), (3, 8),
+    (1, 0), (1, 1), (1, 2), (1, 3), (1, 4), (1, 5), (1, 6), (1, 7), (1, 8), (1, 9), (2, [0, 1, 2]), (1, 10), (1,
+    11), (1, 12), (1, 13), (1, 14), (0, 0), (0, 1), (0, 2), (0, 3), (0, 4), (1, 15), (1, 16), (1, 17), (1, 18), (1,
+    19), (1, 20), (2, [3, 4, 5]), (2, [6, 7]), (0, 5), (0, 6), (0, 7), (0, 8), (0, 9), (1, 21), (1, 22), (1, 23),
+    (1, 24), (2, [8, 9, 10]), (2, [11]), (0, 10), (0, 11), (0, 12), (0, 13), (0, 14), (0, 15), (1, 25), (1, 26), (1,
+    27), (2, [12, 13, 14]), (2, [15]), (0, 16), (1, 28), (0, 17), (1, 29), (0, 18), (0, 19), (1, 30), (0, 20), (1,
+    31), (0, 21), (1, 32), (2, [16, 17, 18]), (2, [19]), (0, 22), (1, 33), (0, 23), (1, 34), (0, 24), (0, 25), (1,
+    35), (1, 36), (2, [20, 21, 22]), (0, 26), (0, 28), (0, 27), (0, 29), (0, 30), (2, [23]), (0, 32), (2, [24, 25]),
+    (3, [0]), (2, [26]), (0, 31), (0, 33), (0, 34), (2, [27]), (0, 35), (2, [28, 29]), (3, [12]), (0, 36), (2, [30,
+    31]), (3, [8]), (2, [32, 33, 34]), (3, [2]), (2, [35]), (3, [11, 6, 13, 1]), (2, [36]), (3, [10]), (2, [37,
+    38]), (3, [5, 4, 9, 3, 7]),
 ]
 
 
@@ -169,7 +169,7 @@
     pl.semaphore_wait(barrier, len(DIRECTIONS) + 1)
 
     id_fresh, twin_id_fresh = set(), set()
-    row_touched, col_touched = set(), set()
+    row_touched, col_touched, spread = set(), set(), set()
 
     def piece_copy(index):
         src, dst, piece, direction = SENDS[index]
@@ -185,6 +185,7 @@
             device_at(DIRECTIONS[direction], core),
         )
 
+    as_columns = {(slot, piece) for slot, piece, _ in STEPS}
     first_for = {}
     for index, (src, dst, piece, direction) in enumerate(SENDS):
         first_for.setdefault(dst, index)
@@ -193,11 +194,11 @@
         src, dst, piece, direction = SENDS[index]
         if first_for[dst] == index:
             id_copy(index).wait_recv()
-            ids_to_twin(dst)
+            if dst in {slot for slot, _ in as_columns}:
+                ids_to_twin(dst)
         piece_copy(index).wait_recv()
-        to_twin(dst, piece)
-        if first_for[dst] == index:
-            spread_ids(dst)
+        if (dst, piece) in as_columns:
+            to_twin(dst, piece)
 
     def send(index):
         src, dst, piece, direction = SENDS[index]
@@ -205,39 +206,51 @@
         if first_for[dst] == index:
             start(id_copy(index))
 
-    def step(index):
-        slot, piece, others = STEPS[index]
-        if slot not in twin_id_fresh:
-            twin_id_fresh.add(slot)
-            twin_ids_wait(slot)
-        twin_wait(slot, piece)
+    def step(batch):
+        for index in batch:
+            slot, piece, _ = STEPS[index]
+            if slot not in twin_id_fresh:
+                twin_id_fresh.add(slot)
+                twin_ids_wait(slot)
+            twin_wait(slot, piece)
+
+        @pl.when(core < 2)
+        def _():
+            for index in batch:
+                compare(*STEPS[index])
+
+    def compare(slot, piece, others):
         own = [(0, p) for p in range(PIECES)] if slot == 0 else []
         left = others + own
+        for s in sorted({s for s, _ in left} - spread):
+            spread.add(s)
+            spread_ids(s)
         columns = rows[slot, piece].reshape(2 * PIECE, features)
         stacked = jnp.concatenate([rows[s, p, core] for s, p in left], axis=0)
         scores = lax.dot_general(stacked, columns, NT, preferred_element_type=jnp.float32)
-        for half in range(2):
-            lane_ids = ids[slot, half, :, piece * PIECE:(piece + 1) * PIECE]
-            columns_best = None
-            for at, (s, p) in enumerate(left):
+        lane_ids = [ids[slot, half, :, piece * PIECE:(piece + 1) * PIECE] for half in range(2)]
+        columns_best = [None, None]
+        for at, (s, p) in enumerate(left):
+            row = row_best[s, p] if (s, p) in row_touched else None
+            row_touched.add((s, p))
+            for half in range(2):
                 block = scores[at * PIECE:(at + 1) * PIECE, half * PIECE:(half + 1) * PIECE]
-                allowed = id_rows[s, p] == lane_ids
-                if (s, p) in own and p == piece:
+                allowed = id_rows[s, p] == lane_ids[half]
+                if s == slot and p == piece:
                     r = lax.broadcasted_iota(jnp.int32, (PIECE, PIECE), 0)
                     c = lax.broadcasted_iota(jnp.int32, (PIECE, PIECE), 1)
                     allowed = allowed & (r + PIECE * core != c + PIECE * half)
                 block = jnp.where(allowed, block, NEG)
-                if (s, p) in row_touched:
-                    row_best[s, p] = jnp.maximum(row_best[s, p], block)
-                else:
-                    row_best[s, p] = block
-                    row_touched.add((s, p))
-                if slot != 0:
+                row = block if row is None else jnp.maximum(row, block)
+                if s != slot:
                     best = jnp.max(block.reshape(PIECE // 8, 8, PIECE), axis=0)
-                    columns_best = best if columns_best is None else jnp.maximum(columns_best, best)
-            if columns_best is not None:
-                col_best[slot, piece, half] = columns_best
-                col_touched.add((slot, piece))
+                    seen = columns_best[half]
+                    columns_best[half] = best if seen is None else jnp.maximum(seen, best)
+            row_best[s, p] = row
+        if columns_best[0] is not None:
+            for half in range(2):
+                col_best[slot, piece, half] = columns_best[half]
+            col_touched.add((slot, piece))
 
     def home_copy(slot, to_core):
         if slot == 0:
@@ -250,7 +263,17 @@
             home_recv.at[slot, core], device_at(SLOTS[slot], to_core),
         )
 
-    def go_home(slot):
+    def go_home(slots_done):
+        @pl.when(core < 2)
+        def _():
+            for slot in slots_done:
+                sum_up(slot)
+
+        for slot in slots_done:
+            for to_core in range(2 if slot else 1):
+                start(home_copy(slot, to_core))
+
+    def sum_up(slot):
         for piece in range(PIECES):
             mine = None
             if (slot, piece) in row_touched:
@@ -262,20 +285,11 @@
                 if (slot, piece) in col_touched:
                     best = jnp.maximum(best, jnp.max(col_best[slot, piece, half], axis=0, keepdims=True))
                 partial[slot, half, :, piece * PIECE:(piece + 1) * PIECE] = best
-        if slot == 0:
-            start(home_copy(0, None))
-        else:
-            for to_core in range(2):
-                start(home_copy(slot, to_core))
 
     for piece in range(PIECES):
         to_twin(0, piece)
     ids_to_twin(0)
-    spread = False
     for kind, index in ORDER:
-        if kind == 2 and not spread:
-            spread = True
-            spread_ids(0)
         (arrive, send, step, go_home)[kind](index)
 
     best = partial[0, core]

time: 53.5 us -> 44 us (0.82)
  Pallas kernels: 52.1 us -> 42.6 us
    pallas_call x1, Pallas kernels: 52.1 us -> 42.6 us  [local(): pl.pallas_call(kernel, out_shape=jax.ShapeDtypeStruct((1, count), jnp.flo...]
where the time goes in v2:
time: 44 us; the launch traced here: 43.9 us
  Pallas kernels  42.6 us (97%)
  other arithmetic  1.28 us (3%)
    pallas_call x1, Pallas kernels, local(): pl.pallas_call(kernel, out_shape=jax.ShapeDtypeStruct((1, count), jnp.flo...  42.6 us
    pallas_call x1, other arithmetic, local(): pl.pallas_call(kernel, out_shape=jax.ShapeDtypeStruct((1, count), jnp.flo...  1.28 us

profile of v2, /device:TPU:1, one launch (start us, length us, event | category | flops | bytes accessed | tf_op | source)
XLA Modules:
  0.0 43.9 jit_solution(5931955689346993925)
XLA Ops:
  0.0 42.6 %shard_map.28 = f32[1,384]{1,0:T(1,128)} custom-call(bf16[384,512]{1,0:T(8,128)(2,1)} %x_ref.1, s32[1,384]{1,0:T(1,128)} %bitcast.1), custom_call_target="tpu_custom_call" | custom-call | tf_op jit(solution)/shard_map/pallas_call | solution.py:316
  42.6 1.3 %reduce = f32[384]{0:T(512)} reduce(f32[1,384]{1,0:T(1,128)} %shard_map.28, f32[]{:T(128)} %constant), dimensions={0}, to_apply=%pallas_call.3.reduce_sub_computation | reduce | bytes 3076 | tf_op jit(solution)/shard_map/pallas_call | solution.py:316

commit v3 on v2

v3 whole, which is shorter than its diff:
```python
import jax
import jax.numpy as jnp
from jax import lax
from jax.experimental import pallas as pl
from jax.experimental.pallas import tpu as pltpu
from jax.sharding import PartitionSpec as P

MESH = pl.DeviceIdType.MESH
NT = (((1,), (1,)), ((), ()))
NEG = float("-inf")
PIECES = 3
PIECE = 128
DIRECTIONS = [(1, 0, 0), (-1, 0, 0), (0, 1, 0), (0, -1, 0), (0, 0, 1), (0, 0, -1)]
TWIST = 0
SLOTS = [
    (0, 0, 0), (0, 0, 1), (0, 0, 2), (0, 0, 3), (0, 1, 0), (0, 3, 0), (0, 3, 1), (0, 3, 2), (0, 3, 3), (1, 0, 0),
    (2, 0, 0), (2, 1, 0), (3, 0, 0), (3, 1, 0),
]
SENDS = [
    (0, 12, 1, 0), (0, 9, 0, 1), (0, 5, 0, 2), (0, 4, 2, 3), (0, 3, 2, 4), (0, 1, 1, 5), (0, 12, 0, 0), (0, 9, 2,
    1), (0, 5, 2, 2), (0, 4, 1, 3), (0, 3, 1, 4), (0, 1, 0, 5), (0, 12, 2, 0), (0, 9, 1, 1), (0, 4, 0, 3), (0, 1, 2,
    5), (5, 8, 0, 4), (3, 8, 2, 2), (4, 13, 2, 0), (9, 10, 0, 1), (1, 6, 1, 2), (12, 13, 1, 3), (3, 2, 2, 4), (1, 2,
    1, 5), (12, 10, 1, 0), (9, 10, 2, 1), (3, 8, 1, 2), (12, 13, 0, 3), (1, 2, 0, 5), (8, 7, 2, 4), (13, 11, 2, 0),
    (1, 6, 0, 2), (8, 7, 0, 4), (10, 11, 0, 3), (6, 7, 1, 5), (13, 11, 1, 0), (1, 6, 2, 2), (8, 5, 1, 5),
]
STEPS = [
    (0, 0, []),
    (0, 1, []),
    (0, 2, []),
    (12, 1, [(0, 0), (0, 1), (0, 2), (1, 1), (3, 2), (4, 2), (5, 0), (9, 0)]),
    (5, 0, [(0, 0), (0, 1), (0, 2), (1, 1), (3, 2), (4, 2), (9, 0)]),
    (9, 0, [(0, 0), (0, 2), (1, 1), (3, 2), (4, 2)]),
    (3, 2, [(0, 0), (0, 1), (0, 2), (1, 1), (4, 2)]),
    (4, 2, [(0, 1), (0, 2), (1, 1), (3, 1), (5, 2), (9, 2), (12, 0)]),
    (1, 1, [(0, 0), (0, 1), (3, 1), (4, 1), (5, 2), (12, 0)]),
    (12, 0, [(0, 1), (0, 2), (1, 0), (3, 1), (3, 2), (4, 1), (5, 0), (5, 2), (9, 0), (9, 2)]),
    (5, 2, [(0, 0), (0, 1), (1, 0), (3, 1), (3, 2), (4, 1), (9, 0), (9, 2), (12, 1)]),
    (9, 2, [(0, 2), (3, 1), (3, 2), (12, 1)]),
    (1, 0, [(0, 0), (0, 1), (3, 1), (3, 2), (4, 0), (4, 1), (5, 0), (8, 0), (8, 2), (9, 0), (12, 1)]),
    (4, 1, [(0, 1), (3, 1), (5, 0), (8, 0), (8, 2), (9, 1), (12, 1), (12, 2)]),
    (3, 1, [(0, 2), (4, 0), (12, 1), (12, 2)]),
    (8, 0, [(0, 2), (1, 1), (1, 2), (4, 0), (4, 2), (5, 2), (9, 0), (9, 1), (9, 2), (12, 0), (12, 1), (12, 2)]),
    (8, 2, [(1, 1), (1, 2), (4, 0), (4, 2), (9, 0), (9, 1), (9, 2), (12, 0), (12, 1), (12, 2)]),
    (4, 0, [(0, 1), (1, 1), (1, 2), (5, 0), (9, 1), (12, 1)]),
    (9, 1, [(0, 2), (2, 1), (2, 2), (3, 2), (4, 2), (6, 1), (12, 1), (13, 1), (13, 2)]),
    (1, 2, [(3, 2), (9, 0), (9, 2), (10, 0), (12, 0), (13, 1), (13, 2)]),
    (10, 0, [(1, 0), (1, 1), (2, 1), (2, 2), (3, 1), (3, 2), (4, 0), (4, 1), (4, 2), (5, 2), (6, 1), (8, 0), (8, 2)]),
    (13, 2, [(1, 0), (1, 1), (2, 1), (2, 2), (3, 1), (5, 0), (5, 2), (6, 1), (8, 0), (8, 2), (9, 2)]),
    (13, 1, [(1, 0), (1, 1), (2, 0), (2, 1), (2, 2), (3, 1), (5, 0), (5, 2), (6, 1), (7, 2), (8, 0), (8, 1), (8, 2), (9, 2)]),
    (6, 1, [(3, 1), (3, 2), (4, 1), (9, 0), (9, 2), (10, 1), (10, 2), (12, 0), (13, 0)]),
    (2, 2, [(9, 0), (9, 2), (10, 1), (10, 2), (12, 0), (12, 1), (13, 0)]),
    (2, 1, [(4, 0), (9, 0), (10, 1), (12, 0), (13, 0)]),
    (8, 1, [(4, 0), (4, 2), (9, 0), (9, 1), (9, 2), (10, 0), (10, 1), (10, 2), (12, 0), (13, 0), (13, 2)]),
    (7, 2, [(4, 0), (4, 1), (4, 2), (9, 0), (9, 1), (9, 2), (10, 0), (10, 1), (10, 2), (13, 0), (13, 2)]),
    (10, 1, [(1, 1), (1, 2), (3, 2), (4, 0), (6, 0), (7, 0), (7, 1), (8, 0), (8, 2)]),
    (13, 0, [(1, 0), (1, 2), (2, 0), (5, 0), (5, 2), (6, 0), (7, 0), (7, 1), (8, 0), (8, 2)]),
    (10, 2, [(0, 2), (1, 2), (6, 0), (7, 0), (7, 1), (8, 0), (8, 2)]),
    (2, 0, [(0, 0), (9, 0), (10, 0), (11, 0), (13, 2)]),
    (11, 0, [(1, 0), (1, 2), (2, 1), (5, 0), (5, 2), (6, 0), (6, 1), (7, 0), (7, 1), (7, 2), (8, 1), (8, 2)]),
    (11, 2, [(1, 2), (5, 2), (6, 1), (7, 1), (7, 2), (8, 0), (8, 1), (8, 2)]),
    (7, 0, [(4, 0), (4, 1), (9, 0), (9, 1), (9, 2), (13, 1), (13, 2)]),
    (7, 1, [(4, 1), (9, 0), (9, 1), (9, 2), (11, 1), (13, 1), (13, 2)]),
    (6, 0, [(9, 0), (9, 1), (9, 2), (13, 1), (13, 2)]),
    (11, 1, [(1, 2), (5, 0), (5, 1), (5, 2), (6, 1)]),
    (6, 2, [(9, 0), (9, 1), (9, 2), (13, 0), (13, 1), (13, 2)]),
    (5, 1, [(4, 1), (13, 0), (13, 1), (13, 2)]),
]
ORDER = [
    (1, 0),
    (1, 1),
    (1, 2),
    (1, 3),
    (1, 4),
    (1, 5),
    (1, 6),
    (1, 7),
    (1, 8),
    (1, 9),
    (1, 10),
    (1, 11),
    (2, ([0, 1, 2], [], [])),
    (1, 12),
    (1, 13),
    (1, 14),
    (1, 15),
    (0, 0),
    (0, 1),
    (0, 2),
    (1, 16),
    (0, 3),
    (0, 4),
    (1, 17),
    (0, 5),
    (1, 18),
    (1, 19),
    (1, 20),
    (1, 21),
    (1, 22),
    (1, 23),
    (2, ([3], [], [])),
    (2, ([4, 5, 6], [], [])),
    (0, 6),
    (0, 7),
    (0, 8),
    (0, 9),
    (0, 10),
    (0, 11),
    (2, ([7, 8], [], [])),
    (1, 24),
    (1, 25),
    (1, 26),
    (1, 27),
    (1, 28),
    (2, ([9, 10, 11], [], [])),
    (0, 12),
    (0, 13),
    (0, 14),
    (0, 17),
    (1, 29),
    (0, 16),
    (0, 15),
    (2, ([12, 13, 14], [], [])),
    (2, ([15, 16, 17], [], [])),
    (0, 18),
    (1, 30),
    (1, 31),
    (1, 32),
    (0, 19),
    (1, 33),
    (0, 20),
    (1, 34),
    (0, 21),
    (0, 22),
    (0, 23),
    (2, ([18, 19], [], [])),
    (2, ([20, 21], [], [])),
    (0, 24),
    (1, 35),
    (1, 36),
    (0, 25),
    (0, 26),
    (1, 37),
    (0, 27),
    (0, 29),
    (0, 28),
    (2, ([22, 23, 24], [], [])),
    (2, ([25, 26, 27], [], [])),
    (0, 30),
    (0, 31),
    (0, 32),
    (0, 33),
    (0, 34),
    (2, ([28, 29, 30], [12], [])),
    (2, ([31, 32, 33], [3], [])),
    (0, 35),
    (0, 36),
    (0, 37),
    (2, ([34, 35, 36], [10, 2, 8, 0], [])),
    (2, ([37], [7], [])),
    (2, ([38, 39], [11, 1], [6, 13, 9, 4, 5])),
]


def device_at(offset, core):
    cluster = lax.axis_index("cluster")
    blk = lax.axis_index("blk")
    x, y, z = blk % 4, cluster // 2, (cluster % 2) * 2 + blk // 4
    odd = z % 2
    dx, dy, dz = offset
    if TWIST == 1:
        dx, dy = dx - odd * (dx + dy), dy - odd * (dx + dy)
    elif TWIST == 2:
        dx, dy = dx + odd * (dy - dx), dy + odd * (dx - dy)
    elif TWIST == 3:
        dx, dy = dx - odd * (2 * dx), dy - odd * (2 * dy)
    elif TWIST == 4:
        dx = dx - odd * (2 * dx)
    x, y, z = (x + dx + 8) % 4, (y + dy + 8) % 4, (z + dz + 8) % 4
    return (y * 2 + z // 2, core, (z % 2) * 4 + x)


def send_groups():
    slots = len(SLOTS)
    columns = {(slot, piece) for slot, piece, _ in STEPS}
    pieces = len(SENDS) + len(columns)
    single_rows = len({dst for _, dst, _, _ in SENDS}) + len({slot for slot, _ in columns}) + 2 * slots - 1
    groups = []
    for count, each in ((pieces, 2 * PIECES), (single_rows, 2)):
        sizes = []
        while count >= each:
            sizes.append(min(count // each, slots) * each)
            count -= sizes[-1]
        groups.append(sizes + [1] * count)
    return groups


def kernel(
    x_ref, id_ref, o_ref, x_in, id_in, rows, ids, id_rows, row_best, col_best, partial, returned,
    load_sem, sent, sent_small, recv_sem, id_recv, twin_recv, twin_id_recv, home_recv,
):
    core = lax.axis_index("col")
    twin = 1 - core
    here = (0, 0, 0)
    slots = len(SLOTS)

    barrier = pltpu.get_barrier_semaphore()
    for direction in DIRECTIONS:
        pl.semaphore_signal(barrier, inc=1, device_id=device_at(direction, core), device_id_type=MESH)
    pl.semaphore_signal(barrier, inc=1, device_id=device_at(here, twin), device_id_type=MESH)
    load = pltpu.make_async_copy(x_ref, x_in, load_sem.at[0])
    load_ids = pltpu.make_async_copy(id_ref, id_in, load_sem.at[1])
    load.start()
    load_ids.start()

    def remote(src, dst, send, recv, device):
        return pltpu.make_async_remote_copy(
            src_ref=src, dst_ref=dst, send_sem=send, recv_sem=recv, device_id=device, device_id_type=MESH
        )

    def spread_ids(slot):
        for piece in range(PIECES):
            lane_ids = ids[slot, core, :, piece * PIECE:(piece + 1) * PIECE]
            id_rows[slot, piece] = jnp.broadcast_to(lane_ids, (PIECE, PIECE)).T

    piece_groups, row_groups = send_groups()
    piece_sems = iter([sent.at[g] for g, size in enumerate(piece_groups) for _ in range(size)])
    row_sems = iter([sent_small.at[g] for g, size in enumerate(row_groups) for _ in range(size)])

    def to_twin(slot, piece):
        copy = remote(
            rows.at[slot, piece, core], rows.at[slot, piece, core],
            next(piece_sems), twin_recv.at[slot, piece], device_at(here, twin),
        )
        copy.start()

    def ids_to_twin(slot):
        copy = remote(
            ids.at[slot, core], ids.at[slot, core], next(row_sems), twin_id_recv.at[slot],
            device_at(here, twin),
        )
        copy.start()

    def twin_wait(slot, piece):
        remote(
            rows.at[slot, piece, twin], rows.at[slot, piece, twin],
            sent.at[0], twin_recv.at[slot, piece], device_at(here, twin),
        ).wait_recv()

    def twin_ids_wait(slot):
        remote(
            ids.at[slot, twin], ids.at[slot, twin], sent_small.at[0], twin_id_recv.at[slot],
            device_at(here, twin),
        ).wait_recv()

    load_ids.wait()
    ids[0, core] = id_in[...].astype(jnp.float32)
    load.wait()
    features = x_in.shape[1]
    for piece in range(PIECES):
        values = x_in[piece * PIECE:(piece + 1) * PIECE].astype(jnp.float32)
        mean = jnp.mean(values * values, axis=-1, keepdims=True)
        scale = lax.rsqrt(mean + 1e-06) * (1.0 / features**0.5)
        rows[0, piece, core] = (values * scale).astype(jnp.bfloat16)
    pl.semaphore_wait(barrier, len(DIRECTIONS) + 1)

    twin_id_fresh = set()
    row_touched, col_touched, spread = set(), set(), set()

    def piece_copy(index, semaphore):
        src, dst, piece, direction = SENDS[index]
        return remote(
            rows.at[src, piece, core], rows.at[dst, piece, core],
            semaphore, recv_sem.at[dst, piece], device_at(DIRECTIONS[direction], core),
        )

    def id_copy(index, semaphore):
        src, dst, piece, direction = SENDS[index]
        return remote(
            ids.at[src, core], ids.at[dst, core], semaphore, id_recv.at[dst],
            device_at(DIRECTIONS[direction], core),
        )

    as_columns = {(slot, piece) for slot, piece, _ in STEPS}
    first_for = {}
    for kind, what in ORDER:
        if kind == 0:
            first_for.setdefault(SENDS[what][1], what)

    def arrive(index):
        src, dst, piece, direction = SENDS[index]
        if first_for[dst] == index:
            id_copy(index, sent_small.at[0]).wait_recv()
            if dst in {slot for slot, _ in as_columns}:
                ids_to_twin(dst)
        piece_copy(index, sent.at[0]).wait_recv()
        if (dst, piece) in as_columns:
            to_twin(dst, piece)

    def send(index):
        src, dst, piece, direction = SENDS[index]
        piece_copy(index, next(piece_sems)).start()
        if first_for[dst] == index:
            id_copy(index, next(row_sems)).start()

    def step(work):
        batch, before, after = work
        for index in batch:
            slot, piece, _ = STEPS[index]
            if slot not in twin_id_fresh:
                twin_id_fresh.add(slot)
                twin_ids_wait(slot)
            twin_wait(slot, piece)

        @pl.when(core < 2)
        def _():
            for slot in before:
                sum_up(slot)
            for index in batch:
                compare(*STEPS[index])
            for slot in after:
                sum_up(slot)

        for slot in before + after:
            for to_core in range(2 if slot else 1):
                home_copy(slot, to_core).start()

    def compare(slot, piece, others):
        own = [(0, p) for p in range(PIECES)] if slot == 0 else []
        pieces = others + own
        for s in sorted({s for s, _ in pieces} - spread):
            spread.add(s)
            spread_ids(s)
        columns = rows[slot, piece].reshape(2 * PIECE, features)
        stacked = jnp.concatenate([rows[s, p, core] for s, p in pieces], axis=0)
        scores = lax.dot_general(stacked, columns, NT, preferred_element_type=jnp.float32)
        lane_ids = [ids[slot, half, :, piece * PIECE:(piece + 1) * PIECE] for half in range(2)]
        columns_best = [None, None]
        for at, (s, p) in enumerate(pieces):
            row = row_best[s, p] if (s, p) in row_touched else None
            row_touched.add((s, p))
            for half in range(2):
                block = scores[at * PIECE:(at + 1) * PIECE, half * PIECE:(half + 1) * PIECE]
                allowed = id_rows[s, p] == lane_ids[half]
                if s == slot and p == piece:
                    r = lax.broadcasted_iota(jnp.int32, (PIECE, PIECE), 0)
                    c = lax.broadcasted_iota(jnp.int32, (PIECE, PIECE), 1)
                    allowed = allowed & (r + PIECE * core != c + PIECE * half)
                block = jnp.where(allowed, block, NEG)
                row = block if row is None else jnp.maximum(row, block)
                if s != slot:
                    best = jnp.max(block.reshape(PIECE // 8, 8, PIECE), axis=0)
                    seen = columns_best[half]
                    columns_best[half] = best if seen is None else jnp.maximum(seen, best)
            row_best[s, p] = row
        if columns_best[0] is not None:
            for half in range(2):
                col_best[slot, piece, half] = columns_best[half]
            col_touched.add((slot, piece))

    def home_copy(slot, to_core):
        if slot == 0:
            target, semaphore, device = returned.at[0, core], home_recv.at[0], device_at(here, twin)
            return remote(partial.at[0, twin], target, next(row_sems), semaphore, device)
        target, semaphore, device = returned.at[slot, core], home_recv.at[1], device_at(SLOTS[slot], to_core)
        return remote(partial.at[slot, to_core], target, next(row_sems), semaphore, device)

    def sum_up(slot):
        for piece in range(PIECES):
            mine = None
            if (slot, piece) in row_touched:
                mine = jnp.max(row_best[slot, piece].T, axis=0, keepdims=True)
            for half in range(2):
                best = jnp.full((1, PIECE), NEG, jnp.float32)
                if mine is not None:
                    best = jnp.where(core == half, mine, best)
                if (slot, piece) in col_touched:
                    best = jnp.maximum(best, jnp.max(col_best[slot, piece, half], axis=0, keepdims=True))
                partial[slot, half, :, piece * PIECE:(piece + 1) * PIECE] = best

    for piece in range(PIECES):
        to_twin(0, piece)
    ids_to_twin(0)
    for kind, what in ORDER:
        (arrive, send, step)[kind](what)

    def arrived(array, semaphore):
        remote(array, array, sent.at[0], semaphore, device_at(here, twin)).wait_recv()

    def left(array, semaphore):
        remote(array, array, semaphore, home_recv.at[0], device_at(here, twin)).wait_send()

    returned[0, core] = partial[0, core]
    arrived(returned.at[0, twin], home_recv.at[0])
    arrived(returned.at[1:slots], home_recv.at[1])
    o_ref[...] = jnp.max(returned[...], axis=(0, 1))
    for group, size in enumerate(piece_groups):
        whole = size // (2 * PIECES)
        left(rows.at[0:whole] if whole else rows.at[0, 0, 0], sent.at[group])
    for group, size in enumerate(row_groups):
        whole = size // 2
        left(ids.at[0:whole] if whole else ids.at[0, 0], sent_small.at[group])


def local(embeddings, assignment):
    count, features = embeddings.shape
    slots = len(SLOTS)
    dma = pltpu.SemaphoreType.DMA
    piece_groups, row_groups = send_groups()
    best = pl.pallas_call(
        kernel,
        out_shape=jax.ShapeDtypeStruct((1, count), jnp.float32),
        in_specs=[pl.BlockSpec(memory_space=pl.ANY)] * 2,
        out_specs=pl.BlockSpec(memory_space=pltpu.VMEM),
        scratch_shapes=[
            pltpu.VMEM((count, features), jnp.bfloat16),
            pltpu.VMEM((1, count), jnp.int32),
            pltpu.VMEM((slots, PIECES, 2, PIECE, features), jnp.bfloat16),
            pltpu.VMEM((slots, 2, 1, count), jnp.float32),
            pltpu.VMEM((slots, PIECES, PIECE, PIECE), jnp.float32),
            pltpu.VMEM((slots, PIECES, PIECE, PIECE), jnp.float32),
            pltpu.VMEM((slots, PIECES, 2, 8, PIECE), jnp.float32),
            pltpu.VMEM((slots, 2, 1, count), jnp.float32),
            pltpu.VMEM((slots, 2, 1, count), jnp.float32),
            dma((2,)),
            dma((len(piece_groups),)),
            dma((len(row_groups),)),
            dma((slots, PIECES)),
            dma((slots,)),
            dma((slots, PIECES)),
            dma((slots,)),
            dma((2,)),
        ],
        compiler_params=pltpu.CompilerParams(
            collective_id=0, has_side_effects=True, vmem_limit_bytes=56 * 2**20
        ),
    )(embeddings, assignment.reshape(1, count))
    return best.reshape(count)


def solution(mesh):
    axes = ("cluster", "col", "blk")
    return jax.shard_map(
        local, mesh=mesh, in_specs=(P(axes, None), P(axes, None)), out_specs=P(axes), check_vma=False
    )
```

time: 44 us -> 39.6 us (0.900)
  Pallas kernels: 42.6 us -> 38.2 us
    pallas_call x1, Pallas kernels: 42.6 us -> 38.2 us  [local(): pl.pallas_call(kernel, out_shape=jax.ShapeDtypeStruct((1, count), jnp.flo...]
where the time goes in v3:
time: 39.6 us; the launch traced here: 39.5 us
  Pallas kernels  38.2 us (96%)
  other arithmetic  1.28 us (3%)
    pallas_call x1, Pallas kernels, local(): pl.pallas_call(kernel, out_shape=jax.ShapeDtypeStruct((1, count), jnp.flo...  38.2 us
    pallas_call x1, other arithmetic, local(): pl.pallas_call(kernel, out_shape=jax.ShapeDtypeStruct((1, count), jnp.flo...  1.28 us

profile of v3, /device:TPU:1, one launch (start us, length us, event | category | flops | bytes accessed | tf_op | source)
XLA Modules:
  0.0 39.5 jit_solution(2953649732248060737)
XLA Ops:
  0.0 38.2 %shard_map.28 = f32[1,384]{1,0:T(1,128)} custom-call(bf16[384,512]{1,0:T(8,128)(2,1)} %x_ref.1, s32[1,384]{1,0:T(1,128)} %bitcast.1), custom_call_target="tpu_custom_call" | custom-call | tf_op jit(solution)/shard_map/pallas_call | solution.py:409
  38.2 1.3 %reduce = f32[384]{0:T(512)} reduce(f32[1,384]{1,0:T(1,128)} %shard_map.28, f32[]{:T(128)} %constant), dimensions={0}, to_apply=%pallas_call.3.reduce_sub_computation | reduce | bytes 3076 | tf_op jit(solution)/shard_map/pallas_call | solution.py:409

commit v4 on v3

v4 whole, which is shorter than its diff:
```python
import jax
import jax.numpy as jnp
from jax import lax
from jax.experimental import pallas as pl
from jax.experimental.pallas import tpu as pltpu
from jax.sharding import PartitionSpec as P

MESH = pl.DeviceIdType.MESH
NT = (((1,), (1,)), ((), ()))
NEG = float("-inf")
PIECES = 3
PIECE = 128
DIRECTIONS = [(1, 0, 0), (-1, 0, 0), (0, 1, 0), (0, -1, 0), (0, 0, 1), (0, 0, -1)]
TWIST = 0
SLOTS = [
    (0, 0, 0), (0, 0, 1), (0, 0, 2), (0, 0, 3), (0, 1, 0), (0, 2, 0), (1, 0, 0), (1, 0, 2), (1, 0, 3), (3, 0, 0),
    (3, 1, 0), (3, 2, 0), (3, 3, 0),
]
SENDS = [
    (0, 9, 2, 0), (0, 6, 0, 1), (0, 4, 2, 3), (0, 3, 2, 4), (0, 1, 4, 5), (0, 9, 3, 0), (0, 6, 1, 1), (0, 4, 3, 3),
    (0, 3, 3, 4), (0, 1, 5, 5), (0, 9, 4, 0), (0, 6, 2, 1), (0, 4, 0, 3), (0, 3, 4, 4), (0, 1, 0, 5), (0, 9, 5, 0),
    (0, 6, 3, 1), (0, 4, 1, 3), (0, 3, 5, 4), (0, 1, 1, 5), (0, 9, 0, 0), (0, 6, 4, 1), (0, 4, 4, 3), (0, 3, 0, 4),
    (0, 1, 2, 5), (9, 12, 2, 2), (4, 10, 2, 0), (0, 6, 5, 1), (4, 5, 2, 3), (0, 3, 1, 4), (0, 1, 3, 5), (9, 12, 3,
    2), (4, 10, 3, 0), (3, 8, 2, 1), (4, 5, 3, 3), (6, 8, 0, 4), (1, 2, 4, 5), (9, 12, 4, 2), (4, 10, 0, 0), (3, 8,
    3, 1), (4, 5, 0, 3), (6, 8, 1, 4), (1, 2, 5, 5), (9, 12, 5, 2), (4, 10, 1, 0), (3, 8, 4, 1), (4, 5, 1, 3), (1,
    2, 0, 5), (9, 12, 0, 2), (4, 10, 4, 0), (3, 8, 5, 1), (12, 11, 4, 2), (4, 5, 4, 3), (1, 2, 1, 5), (0, 9, 1, 0),
    (12, 11, 5, 2), (9, 10, 5, 3), (1, 2, 2, 5), (8, 7, 2, 4), (8, 7, 0, 4), (2, 7, 4, 1), (12, 11, 0, 2), (10, 11,
    2, 3), (1, 2, 3, 5), (8, 7, 3, 4), (2, 7, 5, 1), (10, 11, 3, 3), (8, 7, 1, 4), (5, 11, 1, 0), (11, 5, 5, 1), (0,
    4, 5, 3), (9, 12, 1, 2),
]
STEPS = [
    (0, 0, []),
    (0, 1, []),
    (0, 2, []),
    (9, 1, [(0, 0), (0, 1), (0, 2), (1, 2), (3, 1), (4, 1), (6, 0)]),
    (4, 1, [(0, 0), (0, 1), (0, 2), (1, 2), (3, 1), (6, 0)]),
    (3, 1, [(0, 0), (0, 1), (0, 2), (1, 2), (6, 0)]),
    (6, 0, [(0, 0), (0, 2), (1, 0), (1, 2), (3, 2), (4, 0), (9, 2)]),
    (1, 2, [(0, 0), (0, 2), (3, 2), (4, 0), (6, 1), (9, 2)]),
    (6, 1, [(0, 0), (0, 2), (1, 0), (3, 1), (3, 2), (4, 0), (4, 1), (9, 1), (9, 2), (12, 1)]),
    (4, 0, [(0, 0), (0, 1), (0, 2), (1, 0), (3, 1), (3, 2), (9, 1), (9, 2), (12, 1)]),
    (3, 2, [(0, 0), (0, 1), (1, 0), (4, 1), (9, 1), (9, 2), (12, 1)]),
    (1, 0, [(0, 0), (3, 0), (3, 1), (4, 1), (6, 2), (12, 1)]),
    (9, 2, [(0, 2), (4, 1), (6, 2), (12, 1)]),
    (12, 1, [(0, 2), (1, 1), (1, 2), (3, 0), (3, 1), (4, 1), (6, 0), (6, 2)]),
    (3, 0, [(0, 1), (4, 0), (4, 1), (5, 1), (6, 0), (6, 1), (6, 2), (9, 1), (10, 1), (12, 2)]),
    (6, 2, [(0, 0), (4, 0), (4, 1), (5, 1), (10, 1), (12, 2)]),
    (1, 1, [(3, 1), (4, 0), (4, 1), (5, 1), (10, 1), (12, 2)]),
    (12, 2, [(0, 2), (1, 0), (1, 2), (2, 2), (3, 1), (3, 2), (4, 0), (4, 1), (5, 1), (6, 0), (8, 0), (8, 1), (9, 2), (10, 1)]),
    (10, 1, [(1, 0), (1, 2), (2, 2), (3, 1), (3, 2), (6, 0), (8, 0), (8, 1), (12, 1)]),
    (5, 1, [(0, 0), (1, 0), (1, 2), (2, 2), (3, 2), (8, 0), (8, 1)]),
    (8, 1, [(1, 0), (1, 1), (1, 2), (4, 0), (5, 0), (9, 1), (9, 2), (10, 0), (12, 1)]),
    (8, 0, [(1, 0), (1, 1), (1, 2), (4, 0), (5, 0), (9, 1), (9, 2), (10, 0), (12, 1)]),
    (2, 2, [(4, 0), (4, 1), (5, 0), (6, 2), (9, 1), (10, 0), (12, 1)]),
    (5, 0, [(0, 0), (0, 2), (1, 0), (1, 2), (2, 0), (3, 2), (6, 0), (6, 1), (6, 2), (8, 2), (10, 0), (12, 2)]),
    (10, 0, [(1, 0), (1, 1), (1, 2), (2, 0), (3, 2), (5, 1), (6, 0), (8, 2), (11, 2)]),
    (11, 2, [(0, 2), (1, 0), (1, 1), (1, 2), (2, 0), (2, 2), (3, 0), (3, 1), (3, 2), (6, 0), (6, 1), (6, 2), (8, 0), (8, 1), (8, 2), (9, 2)]),
    (8, 2, [(1, 0), (5, 1), (9, 0), (9, 1), (9, 2), (10, 1), (10, 2), (12, 1), (12, 2)]),
    (2, 0, [(4, 0), (4, 1), (5, 1), (10, 1), (10, 2), (11, 0), (12, 1), (12, 2)]),
    (10, 2, [(0, 2), (1, 0), (1, 1), (1, 2), (2, 1), (2, 2), (3, 0), (3, 1), (3, 2), (6, 0), (7, 1), (7, 2), (8, 0), (8, 1)]),
    (9, 0, [(6, 0), (7, 1), (7, 2), (8, 0), (8, 1)]),
    (7, 1, [(4, 0), (4, 1), (5, 0), (5, 1), (5, 2), (9, 1), (9, 2), (10, 0), (10, 1), (11, 0), (11, 1), (11, 2), (12, 2)]),
    (11, 0, [(1, 0), (1, 1), (1, 2), (2, 2), (6, 0), (6, 1), (7, 0), (7, 2), (8, 0), (8, 1), (8, 2)]),
    (2, 1, [(4, 0), (4, 1), (5, 1), (12, 1), (12, 2)]),
    (7, 2, [(5, 1), (9, 2), (10, 0), (11, 2), (12, 0)]),
    (11, 1, [(1, 0), (1, 1), (1, 2), (2, 0), (6, 1), (8, 0), (8, 1), (8, 2)]),
    (7, 0, [(9, 0), (10, 0), (10, 1)]),
    (5, 2, [(1, 2), (2, 2), (10, 0)]),
    (12, 0, [(1, 0), (1, 1), (1, 2), (2, 0), (2, 1), (2, 2), (3, 0), (3, 1), (3, 2), (8, 0), (8, 1), (8, 2)]),
    (4, 2, [(1, 0), (1, 1), (1, 2), (2, 0), (2, 1), (2, 2), (3, 0), (3, 1), (3, 2)]),
]
ORDER = [
    (1, 0),
    (1, 1),
    (1, 2),
    (1, 3),
    (1, 4),
    (1, 5),
    (1, 6),
    (1, 7),
    (1, 8),
    (1, 9),
    (1, 10),
    (1, 11),
    (1, 12),
    (1, 13),
    (1, 14),
    (2, ([0, 1, 2], [], [])),
    (1, 15),
    (1, 16),
    (1, 17),
    (1, 18),
    (1, 19),
    (1, 20),
    (1, 21),
    (1, 22),
    (1, 23),
    (1, 24),
    (0, 0),
    (1, 25),
    (0, 1),
    (0, 2),
    (0, 3),
    (0, 4),
    (1, 26),
    (1, 27),
    (1, 28),
    (1, 29),
    (1, 30),
    (0, 5),
    (1, 31),
    (0, 6),
    (0, 7),
    (0, 8),
    (0, 9),
    (1, 32),
    (1, 33),
    (1, 34),
    (1, 35),
    (1, 36),
    (0, 10),
    (1, 37),
    (0, 11),
    (0, 12),
    (0, 13),
    (0, 14),
    (2, ([3, 4, 5], [], [])),
    (0, 25),
    (1, 38),
    (1, 39),
    (1, 40),
    (1, 41),
    (1, 42),
    (0, 15),
    (1, 43),
    (0, 16),
    (0, 17),
    (0, 18),
    (0, 19),
    (2, ([6, 7], [], [])),
    (1, 44),
    (1, 45),
    (0, 31),
    (1, 46),
    (1, 47),
    (0, 20),
    (1, 48),
    (0, 21),
    (0, 22),
    (0, 23),
    (0, 24),
    (2, ([8, 9, 10], [], [])),
    (0, 37),
    (1, 49),
    (1, 50),
    (1, 51),
    (1, 52),
    (1, 53),
    (0, 26),
    (0, 27),
    (0, 28),
    (0, 29),
    (0, 30),
    (2, ([11, 12, 13], [], [])),
    (0, 43),
    (1, 54),
    (1, 55),
    (1, 56),
    (1, 57),
    (0, 32),
    (0, 33),
    (1, 58),
    (0, 34),
    (0, 35),
    (1, 59),
    (0, 36),
    (1, 60),
    (2, ([14, 15, 16], [], [])),
    (0, 48),
    (1, 61),
    (1, 62),
    (1, 63),
    (0, 38),
    (0, 39),
    (1, 64),
    (0, 40),
    (0, 41),
    (0, 42),
    (1, 65),
    (2, ([17, 18, 19], [], [])),
    (0, 51),
    (1, 66),
    (1, 67),
    (0, 44),
    (0, 45),
    (0, 46),
    (1, 68),
    (0, 47),
    (2, ([20, 21, 22], [], [])),
    (0, 55),
    (1, 69),
    (1, 70),
    (0, 58),
    (0, 49),
    (0, 50),
    (0, 52),
    (0, 53),
    (2, ([23, 24], [], [])),
    (0, 61),
    (0, 59),
    (0, 54),
    (1, 71),
    (0, 60),
    (0, 56),
    (0, 57),
    (2, ([25, 26], [], [])),
    (0, 64),
    (0, 65),
    (0, 62),
    (0, 63),
    (0, 68),
    (2, ([27, 28, 29], [], [])),
    (0, 67),
    (0, 69),
    (0, 66),
    (2, ([30, 31, 32], [0], [])),
    (0, 71),
    (0, 70),
    (2, ([33, 34, 35], [], [])),
    (2, ([36], [11, 7, 6, 9], [])),
    (2, ([37], [5, 10], [])),
    (2, ([38], [12, 8], [2, 1, 3, 4])),
]


def device_at(offset, core):
    cluster = lax.axis_index("cluster")
    blk = lax.axis_index("blk")
    x, y, z = blk % 4, cluster // 2, (cluster % 2) * 2 + blk // 4
    odd = z % 2
    dx, dy, dz = offset
    if TWIST == 1:
        dx, dy = dx - odd * (dx + dy), dy - odd * (dx + dy)
    elif TWIST == 2:
        dx, dy = dx + odd * (dy - dx), dy + odd * (dx - dy)
    elif TWIST == 3:
        dx, dy = dx - odd * (2 * dx), dy - odd * (2 * dy)
    elif TWIST == 4:
        dx = dx - odd * (2 * dx)
    x, y, z = (x + dx + 8) % 4, (y + dy + 8) % 4, (z + dz + 8) % 4
    return (y * 2 + z // 2, core, (z % 2) * 4 + x)


def send_groups():
    halves = len(SENDS)
    slots = len(SLOTS)
    columns = {(slot, piece) for slot, piece, _ in STEPS}
    pieces = len(columns)
    single_rows = len({dst for _, dst, _, _ in SENDS}) + len({slot for slot, _ in columns}) + 2 * slots - 1
    groups = []
    for count, each in ((pieces, 2 * PIECES), (single_rows, 2), (halves, 4 * PIECES)):
        sizes = []
        while count >= each:
            sizes.append(min(count // each, slots) * each)
            count -= sizes[-1]
        groups.append(sizes + [1] * count)
    return groups


def kernel(
    x_ref, id_ref, o_ref, x_in, id_in, rows, ids, id_rows, row_best, col_best, partial, returned,
    load_sem, sent, sent_small, sent_half, recv_sem, id_recv, twin_recv, twin_id_recv, home_recv,
):
    core = lax.axis_index("col")
    twin = 1 - core
    here = (0, 0, 0)
    neighbours = [device_at(direction, core) for direction in DIRECTIONS]
    other_core = device_at(here, twin)
    slots = len(SLOTS)

    barrier = pltpu.get_barrier_semaphore()
    for device in neighbours + [other_core]:
        pl.semaphore_signal(barrier, inc=1, device_id=device, device_id_type=MESH)
    load = pltpu.make_async_copy(x_ref, x_in, load_sem.at[0])
    load_ids = pltpu.make_async_copy(id_ref, id_in, load_sem.at[1])
    load.start()
    load_ids.start()

    def remote(src, dst, send, recv, device):
        return pltpu.make_async_remote_copy(
            src_ref=src, dst_ref=dst, send_sem=send, recv_sem=recv, device_id=device, device_id_type=MESH
        )

    def spread_ids(slot):
        for piece in range(PIECES):
            lane_ids = ids[slot, core, :, piece * PIECE:(piece + 1) * PIECE]
            id_rows[slot, piece] = jnp.broadcast_to(lane_ids, (PIECE, PIECE)).T

    piece_groups, row_groups, half_groups = send_groups()
    piece_sems = iter([sent.at[g] for g, size in enumerate(piece_groups) for _ in range(size)])
    half_sems = iter([sent_half.at[g] for g, size in enumerate(half_groups) for _ in range(size)])
    row_sems = iter([sent_small.at[g] for g, size in enumerate(row_groups) for _ in range(size)])

    def to_twin(slot, piece):
        copy = remote(
            rows.at[slot, piece, core], rows.at[slot, piece, core],
            next(piece_sems), twin_recv.at[slot, piece], other_core,
        )
        copy.start()

    def ids_to_twin(slot):
        copy = remote(
            ids.at[slot, core], ids.at[slot, core], next(row_sems), twin_id_recv.at[slot],
            other_core,
        )
        copy.start()

    def twin_wait(slot, piece):
        remote(
            rows.at[slot, piece, twin], rows.at[slot, piece, twin],
            sent.at[0], twin_recv.at[slot, piece], other_core,
        ).wait_recv()

    def twin_ids_wait(slot):
        remote(
            ids.at[slot, twin], ids.at[slot, twin], sent_small.at[0], twin_id_recv.at[slot],
            other_core,
        ).wait_recv()

    load_ids.wait()
    ids[0, core] = id_in[...].astype(jnp.float32)
    load.wait()
    features = x_in.shape[1]
    for piece in range(PIECES):
        values = x_in[piece * PIECE:(piece + 1) * PIECE].astype(jnp.float32)
        mean = jnp.mean(values * values, axis=-1, keepdims=True)
        scale = lax.rsqrt(mean + 1e-06) * (1.0 / features**0.5)
        rows[0, piece, core] = (values * scale).astype(jnp.bfloat16)
    pl.semaphore_wait(barrier, len(DIRECTIONS) + 1)

    twin_id_fresh = set()
    row_touched, col_touched, spread = set(), set(), set()

    def half_copy(index, semaphore):
        src, dst, half, direction = SENDS[index]
        place = pl.ds(half % 2 * (PIECE // 2), PIECE // 2)
        return remote(
            rows.at[src, half // 2, core, place], rows.at[dst, half // 2, core, place],
            semaphore, recv_sem.at[dst, half], neighbours[direction],
        )

    def id_copy(index, semaphore):
        src, dst, half, direction = SENDS[index]
        return remote(
            ids.at[src, core], ids.at[dst, core], semaphore, id_recv.at[dst],
            neighbours[direction],
        )

    as_columns = {(slot, piece) for slot, piece, _ in STEPS}
    have = set()
    for_twin = [(0, piece) for piece in range(PIECES)] + [(0, None)]

    def serve_twin():
        while for_twin:
            slot, piece = for_twin.pop(0)
            if piece is None:
                ids_to_twin(slot)
            else:
                to_twin(slot, piece)

    first_for = {}
    for kind, what in ORDER:
        if kind == 0:
            first_for.setdefault(SENDS[what][1], what)

    def arrive(index):
        src, dst, half, direction = SENDS[index]
        if first_for[dst] == index:
            id_copy(index, sent_small.at[0]).wait_recv()
            if dst in {slot for slot, _ in as_columns}:
                for_twin.append((dst, None))
        half_copy(index, sent.at[0]).wait_recv()
        have.add((dst, half))
        if (dst, half ^ 1) in have and (dst, half // 2) in as_columns:
            for_twin.append((dst, half // 2))

    def send(index):
        src, dst, half, direction = SENDS[index]
        half_copy(index, next(half_sems)).start()
        if first_for[dst] == index:
            id_copy(index, next(row_sems)).start()

    def step(work):
        batch, before, after = work
        for index in batch:
            slot, piece, _ = STEPS[index]
            if slot not in twin_id_fresh:
                twin_id_fresh.add(slot)
                twin_ids_wait(slot)
            twin_wait(slot, piece)

        @pl.when(core < 2)
        def _():
            for slot in before:
                sum_up(slot)
            for index in batch:
                compare(*STEPS[index])
            for slot in after:
                sum_up(slot)

        for slot in before + after:
            for to_core in range(2 if slot else 1):
                home_copy(slot, to_core).start()

    def compare(slot, piece, others):
        own = [(0, p) for p in range(PIECES)] if slot == 0 else []
        pieces = others + own
        for s in sorted({s for s, _ in pieces} - spread):
            spread.add(s)
            spread_ids(s)
        columns = rows[slot, piece].reshape(2 * PIECE, features)
        stacked = jnp.concatenate([rows[s, p, core] for s, p in pieces], axis=0)
        scores = lax.dot_general(stacked, columns, NT, preferred_element_type=jnp.float32)
        lane_ids = [ids[slot, half, :, piece * PIECE:(piece + 1) * PIECE] for half in range(2)]
        columns_best = [None, None]
        for at, (s, p) in enumerate(pieces):
            row = row_best[s, p] if (s, p) in row_touched else None
            row_touched.add((s, p))
            for half in range(2):
                block = scores[at * PIECE:(at + 1) * PIECE, half * PIECE:(half + 1) * PIECE]
                allowed = id_rows[s, p] == lane_ids[half]
                if s == slot and p == piece:
                    r = lax.broadcasted_iota(jnp.int32, (PIECE, PIECE), 0)
                    c = lax.broadcasted_iota(jnp.int32, (PIECE, PIECE), 1)
                    allowed = allowed & (r + PIECE * core != c + PIECE * half)
                block = jnp.where(allowed, block, NEG)
                row = block if row is None else jnp.maximum(row, block)
                if s != slot:
                    best = jnp.max(block.reshape(PIECE // 8, 8, PIECE), axis=0)
                    seen = columns_best[half]
                    columns_best[half] = best if seen is None else jnp.maximum(seen, best)
            row_best[s, p] = row
        if columns_best[0] is not None:
            for half in range(2):
                col_best[slot, piece, half] = columns_best[half]
            col_touched.add((slot, piece))

    def home_copy(slot, to_core):
        if slot == 0:
            target, semaphore, device = returned.at[0, core], home_recv.at[0], other_core
            return remote(partial.at[0, twin], target, next(row_sems), semaphore, device)
        target, semaphore, device = returned.at[slot, core], home_recv.at[1], device_at(SLOTS[slot], to_core)
        return remote(partial.at[slot, to_core], target, next(row_sems), semaphore, device)

    def sum_up(slot):
        for piece in range(PIECES):
            mine = None
            if (slot, piece) in row_touched:
                mine = jnp.max(row_best[slot, piece].T, axis=0, keepdims=True)
            for half in range(2):
                best = jnp.full((1, PIECE), NEG, jnp.float32)
                if mine is not None:
                    best = jnp.where(core == half, mine, best)
                if (slot, piece) in col_touched:
                    best = jnp.maximum(best, jnp.max(col_best[slot, piece, half], axis=0, keepdims=True))
                partial[slot, half, :, piece * PIECE:(piece + 1) * PIECE] = best

    for kind, what in ORDER:
        if kind != 1:
            serve_twin()
        (arrive, send, step)[kind](what)

    def arrived(array, semaphore):
        remote(array, array, sent.at[0], semaphore, other_core).wait_recv()

    def left(array, semaphore):
        remote(array, array, semaphore, home_recv.at[0], other_core).wait_send()

    returned[0, core] = partial[0, core]
    arrived(returned.at[0, twin], home_recv.at[0])
    arrived(returned.at[1:slots], home_recv.at[1])
    o_ref[...] = jnp.max(returned[...], axis=(0, 1))
    for group, size in enumerate(piece_groups):
        whole = size // (2 * PIECES)
        left(rows.at[0:whole] if whole else rows.at[0, 0, 0], sent.at[group])
    for group, size in enumerate(half_groups):
        whole = size // (4 * PIECES)
        left(rows.at[0:whole] if whole else rows.at[0, 0, 0, 0:PIECE // 2], sent_half.at[group])
    for group, size in enumerate(row_groups):
        whole = size // 2
        left(ids.at[0:whole] if whole else ids.at[0, 0], sent_small.at[group])


def local(embeddings, assignment):
    count, features = embeddings.shape
    slots = len(SLOTS)
    dma = pltpu.SemaphoreType.DMA
    piece_groups, row_groups, half_groups = send_groups()
    best = pl.pallas_call(
        kernel,
        out_shape=jax.ShapeDtypeStruct((1, count), jnp.float32),
        in_specs=[pl.BlockSpec(memory_space=pl.ANY)] * 2,
        out_specs=pl.BlockSpec(memory_space=pltpu.VMEM),
        scratch_shapes=[
            pltpu.VMEM((count, features), jnp.bfloat16),
            pltpu.VMEM((1, count), jnp.int32),
            pltpu.VMEM((slots, PIECES, 2, PIECE, features), jnp.bfloat16),
            pltpu.VMEM((slots, 2, 1, count), jnp.float32),
            pltpu.VMEM((slots, PIECES, PIECE, PIECE), jnp.float32),
            pltpu.VMEM((slots, PIECES, PIECE, PIECE), jnp.float32),
            pltpu.VMEM((slots, PIECES, 2, 8, PIECE), jnp.float32),
            pltpu.VMEM((slots, 2, 1, count), jnp.float32),
            pltpu.VMEM((slots, 2, 1, count), jnp.float32),
            dma((2,)),
            dma((len(piece_groups),)),
            dma((len(row_groups),)),
            dma((len(half_groups),)),
            dma((slots, 2 * PIECES)),
            dma((slots,)),
            dma((slots, PIECES)),
            dma((slots,)),
            dma((2,)),
        ],
        compiler_params=pltpu.CompilerParams(
            collective_id=0, has_side_effects=True, vmem_limit_bytes=56 * 2**20
        ),
    )(embeddings, assignment.reshape(1, count))
    return best.reshape(count)


def solution(mesh):
    axes = ("cluster", "col", "blk")
    return jax.shard_map(
        local, mesh=mesh, in_specs=(P(axes, None), P(axes, None)), out_specs=P(axes), check_vma=False
    )
```

time: 39.6 us -> 39.3 us (level)
  no operation moved by 1% of the time
where the time goes in v4:
time: 39.3 us; the launch traced here: 39.2 us
  Pallas kernels  37.9 us (96%)
  other arithmetic  1.28 us (3%)
    pallas_call x1, Pallas kernels, local(): pl.pallas_call(kernel, out_shape=jax.ShapeDtypeStruct((1, count), jnp.flo...  37.9 us
    pallas_call x1, other arithmetic, local(): pl.pallas_call(kernel, out_shape=jax.ShapeDtypeStruct((1, count), jnp.flo...  1.28 us

profile of v4, /device:TPU:1, one launch (start us, length us, event | category | flops | bytes accessed | tf_op | source)
XLA Modules:
  0.0 39.2 jit_solution(15893298174627293716)
XLA Ops:
  0.0 37.9 %shard_map.28 = f32[1,384]{1,0:T(1,128)} custom-call(bf16[384,512]{1,0:T(8,128)(2,1)} %x_ref.1, s32[1,384]{1,0:T(1,128)} %bitcast.1), custom_call_target="tpu_custom_call" | custom-call | tf_op jit(solution)/shard_map/pallas_call | solution.py:499
  37.9 1.3 %reduce = f32[384]{0:T(512)} reduce(f32[1,384]{1,0:T(1,128)} %shard_map.28, f32[]{:T(128)} %constant), dimensions={0}, to_apply=%pallas_call.3.reduce_sub_computation | reduce | bytes 3076 | tf_op jit(solution)/shard_map/pallas_call | solution.py:499

commit v5 on v4

--- a/solution.py
+++ b/solution.py
@@ -13,61 +13,62 @@
 DIRECTIONS = [(1, 0, 0), (-1, 0, 0), (0, 1, 0), (0, -1, 0), (0, 0, 1), (0, 0, -1)]
 TWIST = 0
 SLOTS = [
-    (0, 0, 0), (0, 0, 1), (0, 0, 2), (0, 0, 3), (0, 1, 0), (0, 2, 0), (1, 0, 0), (1, 0, 2), (1, 0, 3), (3, 0, 0),
-    (3, 1, 0), (3, 2, 0), (3, 3, 0),
+    (0, 0, 0), (0, 0, 1), (0, 0, 2), (0, 0, 3), (0, 1, 0), (0, 2, 0), (1, 0, 0), (1, 0, 2), (1, 0, 3), (1, 1, 3),
+    (3, 0, 0), (3, 1, 0), (3, 2, 0), (3, 3, 0),
 ]
 SENDS = [
-    (0, 9, 2, 0), (0, 6, 0, 1), (0, 4, 2, 3), (0, 3, 2, 4), (0, 1, 4, 5), (0, 9, 3, 0), (0, 6, 1, 1), (0, 4, 3, 3),
-    (0, 3, 3, 4), (0, 1, 5, 5), (0, 9, 4, 0), (0, 6, 2, 1), (0, 4, 0, 3), (0, 3, 4, 4), (0, 1, 0, 5), (0, 9, 5, 0),
-    (0, 6, 3, 1), (0, 4, 1, 3), (0, 3, 5, 4), (0, 1, 1, 5), (0, 9, 0, 0), (0, 6, 4, 1), (0, 4, 4, 3), (0, 3, 0, 4),
-    (0, 1, 2, 5), (9, 12, 2, 2), (4, 10, 2, 0), (0, 6, 5, 1), (4, 5, 2, 3), (0, 3, 1, 4), (0, 1, 3, 5), (9, 12, 3,
-    2), (4, 10, 3, 0), (3, 8, 2, 1), (4, 5, 3, 3), (6, 8, 0, 4), (1, 2, 4, 5), (9, 12, 4, 2), (4, 10, 0, 0), (3, 8,
-    3, 1), (4, 5, 0, 3), (6, 8, 1, 4), (1, 2, 5, 5), (9, 12, 5, 2), (4, 10, 1, 0), (3, 8, 4, 1), (4, 5, 1, 3), (1,
-    2, 0, 5), (9, 12, 0, 2), (4, 10, 4, 0), (3, 8, 5, 1), (12, 11, 4, 2), (4, 5, 4, 3), (1, 2, 1, 5), (0, 9, 1, 0),
-    (12, 11, 5, 2), (9, 10, 5, 3), (1, 2, 2, 5), (8, 7, 2, 4), (8, 7, 0, 4), (2, 7, 4, 1), (12, 11, 0, 2), (10, 11,
-    2, 3), (1, 2, 3, 5), (8, 7, 3, 4), (2, 7, 5, 1), (10, 11, 3, 3), (8, 7, 1, 4), (5, 11, 1, 0), (11, 5, 5, 1), (0,
-    4, 5, 3), (9, 12, 1, 2),
+    (0, 10, 4, 0), (0, 6, 2, 1), (0, 4, 2, 3), (0, 3, 4, 4), (0, 1, 0, 5), (0, 10, 5, 0), (0, 6, 3, 1), (0, 4, 3,
+    3), (0, 3, 5, 4), (0, 1, 1, 5), (0, 10, 2, 0), (0, 6, 4, 1), (0, 4, 0, 3), (0, 3, 0, 4), (0, 1, 2, 5), (0, 10,
+    3, 0), (0, 6, 5, 1), (0, 4, 1, 3), (0, 3, 1, 4), (0, 1, 3, 5), (0, 10, 0, 0), (0, 6, 0, 1), (0, 4, 4, 3), (0, 1,
+    4, 5), (10, 13, 4, 2), (6, 8, 2, 4), (0, 10, 1, 0), (0, 6, 1, 1), (4, 5, 2, 3), (0, 1, 5, 5), (10, 13, 5, 2),
+    (6, 8, 3, 4), (3, 8, 4, 1), (4, 5, 3, 3), (1, 2, 0, 5), (10, 13, 2, 2), (4, 11, 0, 0), (3, 8, 0, 1), (13, 12, 4,
+    2), (4, 5, 0, 3), (1, 2, 2, 5), (10, 13, 3, 2), (6, 8, 5, 4), (4, 11, 1, 0), (3, 2, 1, 4), (3, 8, 1, 1), (13,
+    12, 5, 2), (4, 5, 1, 3), (1, 2, 3, 5), (4, 11, 4, 0), (8, 7, 2, 4), (10, 13, 0, 2), (8, 9, 2, 3), (1, 2, 4, 5),
+    (5, 12, 2, 0), (8, 7, 3, 4), (12, 5, 4, 1), (10, 13, 1, 2), (8, 9, 3, 3), (1, 2, 5, 5), (8, 7, 4, 4), (5, 12, 3,
+    0), (2, 7, 0, 1), (11, 12, 0, 3), (8, 7, 5, 4), (2, 7, 1, 1), (2, 3, 2, 5), (12, 5, 5, 1), (12, 11, 5, 2), (11,
+    12, 1, 3), (2, 3, 3, 5), (0, 4, 5, 3), (12, 11, 2, 2), (12, 11, 3, 2),
 ]
 STEPS = [
     (0, 0, []),
     (0, 1, []),
     (0, 2, []),
-    (9, 1, [(0, 0), (0, 1), (0, 2), (1, 2), (3, 1), (4, 1), (6, 0)]),
-    (4, 1, [(0, 0), (0, 1), (0, 2), (1, 2), (3, 1), (6, 0)]),
-    (3, 1, [(0, 0), (0, 1), (0, 2), (1, 2), (6, 0)]),
-    (6, 0, [(0, 0), (0, 2), (1, 0), (1, 2), (3, 2), (4, 0), (9, 2)]),
-    (1, 2, [(0, 0), (0, 2), (3, 2), (4, 0), (6, 1), (9, 2)]),
-    (6, 1, [(0, 0), (0, 2), (1, 0), (3, 1), (3, 2), (4, 0), (4, 1), (9, 1), (9, 2), (12, 1)]),
-    (4, 0, [(0, 0), (0, 1), (0, 2), (1, 0), (3, 1), (3, 2), (9, 1), (9, 2), (12, 1)]),
-    (3, 2, [(0, 0), (0, 1), (1, 0), (4, 1), (9, 1), (9, 2), (12, 1)]),
-    (1, 0, [(0, 0), (3, 0), (3, 1), (4, 1), (6, 2), (12, 1)]),
-    (9, 2, [(0, 2), (4, 1), (6, 2), (12, 1)]),
-    (12, 1, [(0, 2), (1, 1), (1, 2), (3, 0), (3, 1), (4, 1), (6, 0), (6, 2)]),
-    (3, 0, [(0, 1), (4, 0), (4, 1), (5, 1), (6, 0), (6, 1), (6, 2), (9, 1), (10, 1), (12, 2)]),
-    (6, 2, [(0, 0), (4, 0), (4, 1), (5, 1), (10, 1), (12, 2)]),
-    (1, 1, [(3, 1), (4, 0), (4, 1), (5, 1), (10, 1), (12, 2)]),
-    (12, 2, [(0, 2), (1, 0), (1, 2), (2, 2), (3, 1), (3, 2), (4, 0), (4, 1), (5, 1), (6, 0), (8, 0), (8, 1), (9, 2), (10, 1)]),
-    (10, 1, [(1, 0), (1, 2), (2, 2), (3, 1), (3, 2), (6, 0), (8, 0), (8, 1), (12, 1)]),
-    (5, 1, [(0, 0), (1, 0), (1, 2), (2, 2), (3, 2), (8, 0), (8, 1)]),
-    (8, 1, [(1, 0), (1, 1), (1, 2), (4, 0), (5, 0), (9, 1), (9, 2), (10, 0), (12, 1)]),
-    (8, 0, [(1, 0), (1, 1), (1, 2), (4, 0), (5, 0), (9, 1), (9, 2), (10, 0), (12, 1)]),
-    (2, 2, [(4, 0), (4, 1), (5, 0), (6, 2), (9, 1), (10, 0), (12, 1)]),
-    (5, 0, [(0, 0), (0, 2), (1, 0), (1, 2), (2, 0), (3, 2), (6, 0), (6, 1), (6, 2), (8, 2), (10, 0), (12, 2)]),
-    (10, 0, [(1, 0), (1, 1), (1, 2), (2, 0), (3, 2), (5, 1), (6, 0), (8, 2), (11, 2)]),
-    (11, 2, [(0, 2), (1, 0), (1, 1), (1, 2), (2, 0), (2, 2), (3, 0), (3, 1), (3, 2), (6, 0), (6, 1), (6, 2), (8, 0), (8, 1), (8, 2), (9, 2)]),
-    (8, 2, [(1, 0), (5, 1), (9, 0), (9, 1), (9, 2), (10, 1), (10, 2), (12, 1), (12, 2)]),
-    (2, 0, [(4, 0), (4, 1), (5, 1), (10, 1), (10, 2), (11, 0), (12, 1), (12, 2)]),
-    (10, 2, [(0, 2), (1, 0), (1, 1), (1, 2), (2, 1), (2, 2), (3, 0), (3, 1), (3, 2), (6, 0), (7, 1), (7, 2), (8, 0), (8, 1)]),
-    (9, 0, [(6, 0), (7, 1), (7, 2), (8, 0), (8, 1)]),
-    (7, 1, [(4, 0), (4, 1), (5, 0), (5, 1), (5, 2), (9, 1), (9, 2), (10, 0), (10, 1), (11, 0), (11, 1), (11, 2), (12, 2)]),
-    (11, 0, [(1, 0), (1, 1), (1, 2), (2, 2), (6, 0), (6, 1), (7, 0), (7, 2), (8, 0), (8, 1), (8, 2)]),
-    (2, 1, [(4, 0), (4, 1), (5, 1), (12, 1), (12, 2)]),
-    (7, 2, [(5, 1), (9, 2), (10, 0), (11, 2), (12, 0)]),
-    (11, 1, [(1, 0), (1, 1), (1, 2), (2, 0), (6, 1), (8, 0), (8, 1), (8, 2)]),
-    (7, 0, [(9, 0), (10, 0), (10, 1)]),
-    (5, 2, [(1, 2), (2, 2), (10, 0)]),
-    (12, 0, [(1, 0), (1, 1), (1, 2), (2, 0), (2, 1), (2, 2), (3, 0), (3, 1), (3, 2), (8, 0), (8, 1), (8, 2)]),
-    (4, 2, [(1, 0), (1, 1), (1, 2), (2, 0), (2, 1), (2, 2), (3, 0), (3, 1), (3, 2)]),
+    (10, 2, [(0, 0), (0, 1), (0, 2), (1, 0), (3, 2), (4, 1), (6, 1)]),
+    (4, 1, [(0, 0), (0, 1), (0, 2), (1, 0), (3, 2), (6, 1)]),
+    (6, 1, [(0, 0), (0, 1), (1, 0), (3, 2)]),
+    (3, 2, [(0, 0), (0, 1), (0, 2), (1, 0), (1, 1), (4, 0), (6, 2), (10, 1)]),
+    (1, 0, [(0, 0), (0, 1), (3, 0), (4, 0), (6, 2), (10, 1)]),
+    (4, 0, [(0, 0), (0, 1), (0, 2), (1, 1), (3, 0), (6, 1), (6, 2), (10, 1), (10, 2), (13, 2)]),
+    (3, 0, [(0, 1), (0, 2), (1, 1), (4, 1), (6, 1), (6, 2), (10, 1), (10, 2), (13, 2)]),
+    (10, 1, [(0, 0), (0, 2), (1, 1), (4, 1), (6, 1)]),
+    (6, 2, [(0, 0), (4, 1), (8, 1), (10, 0), (10, 2), (13, 2)]),
+    (1, 1, [(0, 1), (4, 1), (6, 1), (8, 1), (13, 2)]),
+    (13, 2, [(0, 2), (1, 0), (1, 2), (3, 2), (4, 1), (6, 0), (6, 1), (8, 1), (10, 2)]),
+    (10, 0, [(0, 0), (1, 0), (3, 0), (4, 0), (4, 1), (5, 1), (6, 0), (6, 1), (8, 1), (8, 2)]),
+    (8, 1, [(0, 2), (1, 0), (1, 2), (4, 0), (4, 1), (5, 1), (10, 1), (10, 2)]),
+    (1, 2, [(3, 2), (4, 0), (4, 1), (5, 1), (8, 2), (10, 1)]),
+    (6, 0, [(2, 0), (4, 0), (4, 1), (5, 1), (11, 0), (13, 1)]),
+    (5, 1, [(0, 0), (0, 1), (0, 2), (1, 0), (1, 1), (2, 0), (3, 0), (3, 2), (6, 1), (6, 2), (8, 2), (13, 2)]),
+    (8, 2, [(1, 0), (1, 1), (4, 0), (4, 1), (10, 1), (10, 2), (11, 0), (13, 1), (13, 2)]),
+    (13, 1, [(0, 2), (1, 0), (1, 1), (1, 2), (2, 0), (2, 1), (3, 0), (3, 2), (6, 1), (6, 2), (8, 0), (8, 1), (10, 2)]),
+    (11, 0, [(1, 0), (1, 1), (1, 2), (2, 0), (2, 1), (3, 0), (8, 0), (8, 1), (12, 2), (13, 2)]),
+    (2, 0, [(4, 0), (4, 1), (5, 0), (10, 1), (10, 2), (12, 2), (13, 2)]),
+    (12, 2, [(0, 2), (1, 0), (1, 1), (1, 2), (2, 1), (3, 0), (3, 2), (4, 0), (6, 0), (6, 1), (6, 2), (7, 1), (8, 0), (8, 1), (8, 2), (10, 2)]),
+    (5, 0, [(0, 0), (1, 0), (1, 2), (3, 2), (6, 0), (6, 2), (7, 1), (8, 0), (8, 1), (8, 2)]),
+    (8, 0, [(4, 1), (5, 1), (10, 0), (10, 1), (10, 2), (13, 2)]),
+    (2, 1, [(0, 1), (4, 0), (4, 1), (5, 1), (12, 1), (13, 0), (13, 2)]),
+    (7, 1, [(4, 1), (9, 1), (10, 0), (10, 1), (10, 2), (11, 0), (12, 1), (13, 0), (13, 1), (13, 2)]),
+    (13, 0, [(0, 2), (1, 0), (1, 1), (1, 2), (2, 0), (2, 2), (3, 0), (3, 2), (6, 1), (6, 2), (7, 0), (7, 2), (8, 0), (8, 1), (8, 2), (9, 1)]),
+    (12, 1, [(1, 0), (1, 1), (1, 2), (2, 0), (2, 2), (6, 0), (6, 1), (7, 0), (8, 0), (8, 1), (8, 2), (9, 1)]),
+    (2, 2, [(4, 0), (4, 1), (5, 0), (5, 1), (5, 2), (11, 0), (11, 2), (12, 0), (12, 2), (13, 1), (13, 2)]),
+    (11, 2, [(0, 2), (1, 0), (1, 1), (1, 2), (2, 0), (2, 1), (3, 0), (3, 1), (3, 2), (7, 1), (7, 2), (8, 0), (8, 1), (8, 2)]),
+    (9, 1, [(0, 0), (0, 1), (0, 2)]),
+    (7, 0, [(4, 1), (5, 0), (10, 0), (10, 2), (12, 0), (12, 2), (13, 2)]),
+    (7, 2, [(4, 1), (10, 2), (12, 2)]),
+    (12, 0, [(1, 0), (1, 1), (1, 2), (6, 0), (8, 0), (8, 2)]),
+    (5, 2, [(1, 2), (8, 1)]),
+    (3, 1, [(4, 0), (4, 2)]),
+    (4, 2, [(1, 0), (1, 1), (1, 2), (2, 0), (2, 1), (2, 2), (3, 0), (3, 2)]),
+    (11, 1, [(1, 0), (1, 1), (1, 2), (8, 0), (8, 2)]),
 ]
 ORDER = [
     (1, 0),
@@ -95,10 +96,10 @@
     (1, 21),
     (1, 22),
     (1, 23),
+    (0, 0),
     (1, 24),
-    (0, 0),
+    (0, 1),
     (1, 25),
-    (0, 1),
     (0, 2),
     (0, 3),
     (0, 4),
@@ -106,130 +107,133 @@
     (1, 27),
     (1, 28),
     (1, 29),
+    (0, 5),
     (1, 30),
-    (0, 5),
+    (0, 6),
     (1, 31),
-    (0, 6),
     (0, 7),
     (0, 8),
     (0, 9),
     (1, 32),
     (1, 33),
     (1, 34),
+    (0, 10),
     (1, 35),
-    (1, 36),
-    (0, 10),
-    (1, 37),
     (0, 11),
     (0, 12),
+    (1, 36),
     (0, 13),
     (0, 14),
     (2, ([3, 4, 5], [], [])),
-    (0, 25),
+    (0, 24),
+    (1, 37),
     (1, 38),
     (1, 39),
     (1, 40),
+    (0, 15),
     (1, 41),
+    (0, 16),
     (1, 42),
-    (0, 15),
+    (0, 17),
     (1, 43),
-    (0, 16),
-    (0, 17),
     (0, 18),
+    (1, 44),
     (0, 19),
     (2, ([6, 7], [], [])),
-    (1, 44),
+    (0, 30),
     (1, 45),
-    (0, 31),
     (1, 46),
     (1, 47),
+    (1, 48),
     (0, 20),
-    (1, 48),
     (0, 21),
     (0, 22),
+    (1, 49),
+    (0, 25),
+    (1, 50),
     (0, 23),
-    (0, 24),
     (2, ([8, 9, 10], [], [])),
-    (0, 37),
-    (1, 49),
-    (1, 50),
+    (0, 35),
     (1, 51),
     (1, 52),
     (1, 53),
     (0, 26),
     (0, 27),
     (0, 28),
+    (1, 54),
+    (0, 31),
+    (1, 55),
     (0, 29),
-    (0, 30),
     (2, ([11, 12, 13], [], [])),
-    (0, 43),
-    (1, 54),
-    (1, 55),
+    (0, 38),
     (1, 56),
     (1, 57),
-    (0, 32),
-    (0, 33),
     (1, 58),
-    (0, 34),
-    (0, 35),
     (1, 59),
     (0, 36),
+    (0, 32),
     (1, 60),
+    (0, 33),
+    (1, 61),
+    (0, 42),
+    (0, 34),
+    (1, 62),
     (2, ([14, 15, 16], [], [])),
+    (0, 41),
+    (1, 63),
+    (1, 64),
+    (0, 43),
+    (0, 37),
+    (0, 39),
+    (0, 44),
+    (1, 65),
+    (0, 40),
+    (1, 66),
+    (2, ([17, 18, 19], [], [])),
+    (0, 46),
+    (1, 67),
+    (1, 68),
+    (1, 69),
+    (0, 49),
+    (0, 45),
+    (0, 47),
+    (0, 50),
     (0, 48),
-    (1, 61),
-    (1, 62),
-    (1, 63),
-    (0, 38),
-    (0, 39),
-    (1, 64),
-    (0, 40),
-    (0, 41),
-    (0, 42),
-    (1, 65),
-    (2, ([17, 18, 19], [], [])),
+    (1, 70),
+    (2, ([20, 21, 22], [], [])),
     (0, 51),
-    (1, 66),
-    (1, 67),
-    (0, 44),
-    (0, 45),
-    (0, 46),
-    (1, 68),
-    (0, 47),
-    (2, ([20, 21, 22], [], [])),
+    (1, 71),
+    (0, 54),
+    (1, 72),
+    (0, 56),
+    (0, 52),
     (0, 55),
-    (1, 69),
-    (1, 70),
+    (0, 53),
+    (2, ([23, 24, 25], [], [])),
+    (0, 57),
+    (0, 61),
+    (1, 73),
+    (0, 62),
     (0, 58),
-    (0, 49),
-    (0, 50),
-    (0, 52),
-    (0, 53),
-    (2, ([23, 24], [], [])),
-    (0, 61),
+    (0, 60),
     (0, 59),
-    (0, 54),
-    (1, 71),
-    (0, 60),
-    (0, 56),
-    (0, 57),
-    (2, ([25, 26], [], [])),
+    (2, ([26, 27], [], [])),
+    (0, 68),
+    (0, 65),
+    (0, 63),
     (0, 64),
-    (0, 65),
-    (0, 62),
-    (0, 63),
-    (0, 68),
-    (2, ([27, 28, 29], [], [])),
+    (0, 66),
+    (2, ([28, 29], [], [])),
     (0, 67),
     (0, 69),
-    (0, 66),
-    (2, ([30, 31, 32], [0], [])),
+    (0, 70),
+    (0, 72),
+    (2, ([30, 31, 32], [], [])),
     (0, 71),
-    (0, 70),
-    (2, ([33, 34, 35], [], [])),
-    (2, ([36], [11, 7, 6, 9], [])),
-    (2, ([37], [5, 10], [])),
-    (2, ([38], [12, 8], [2, 1, 3, 4])),
+    (0, 73),
+    (2, ([33, 34, 35], [9, 0], [])),
+    (2, ([36, 37], [7, 12, 13, 10, 6], [])),
+    (2, ([38, 39], [5], [2, 8, 11, 3, 4, 1])),
 ]
 
 

time: 39.3 us -> 39.3 us (level)
  no operation moved by 1% of the time
where the time goes in v5:
time: 39.3 us; the launch traced here: 39.1 us
  Pallas kernels  37.8 us (96%)
  other arithmetic  1.28 us (3%)
    pallas_call x1, Pallas kernels, local(): pl.pallas_call(kernel, out_shape=jax.ShapeDtypeStruct((1, count), jnp.flo...  37.8 us
    pallas_call x1, other arithmetic, local(): pl.pallas_call(kernel, out_shape=jax.ShapeDtypeStruct((1, count), jnp.flo...  1.28 us

profile of v5, /device:TPU:1, one launch (start us, length us, event | category | flops | bytes accessed | tf_op | source)
XLA Modules:
  0.0 39.1 jit_solution(6142371700643224676)
XLA Ops:
  0.0 37.8 %shard_map.28 = f32[1,384]{1,0:T(1,128)} custom-call(bf16[384,512]{1,0:T(8,128)(2,1)} %x_ref.1, s32[1,384]{1,0:T(1,128)} %bitcast.1), custom_call_target="tpu_custom_call" | custom-call | tf_op jit(solution)/shard_map/pallas_call | solution.py:503
  37.8 1.3 %reduce = f32[384]{0:T(512)} reduce(f32[1,384]{1,0:T(1,128)} %shard_map.28, f32[]{:T(128)} %constant), dimensions={0}, to_apply=%pallas_call.3.reduce_sub_computation | reduce | bytes 3076 | tf_op jit(solution)/shard_map/pallas_call | solution.py:503

commit v6 on v5

--- a/solution.py
+++ b/solution.py
@@ -86,7 +86,7 @@
     (1, 12),
     (1, 13),
     (1, 14),
-    (2, ([0, 1, 2], [], [])),
+    (2, ([0, 1, 2], [(9, 0), (9, 2)], [], [])),
     (1, 15),
     (1, 16),
     (1, 17),
@@ -124,7 +124,7 @@
     (1, 36),
     (0, 13),
     (0, 14),
-    (2, ([3, 4, 5], [], [])),
+    (2, ([3, 4, 5], [], [], [])),
     (0, 24),
     (1, 37),
     (1, 38),
@@ -139,7 +139,7 @@
     (0, 18),
     (1, 44),
     (0, 19),
-    (2, ([6, 7], [], [])),
+    (2, ([6, 7], [], [], [])),
     (0, 30),
     (1, 45),
     (1, 46),
@@ -152,7 +152,7 @@
     (0, 25),
     (1, 50),
     (0, 23),
-    (2, ([8, 9, 10], [], [])),
+    (2, ([8, 9, 10], [], [], [])),
     (0, 35),
     (1, 51),
     (1, 52),
@@ -164,7 +164,7 @@
     (0, 31),
     (1, 55),
     (0, 29),
-    (2, ([11, 12, 13], [], [])),
+    (2, ([11, 12, 13], [], [], [])),
     (0, 38),
     (1, 56),
     (1, 57),
@@ -178,7 +178,7 @@
     (0, 42),
     (0, 34),
     (1, 62),
-    (2, ([14, 15, 16], [], [])),
+    (2, ([14, 15, 16], [], [], [])),
     (0, 41),
     (1, 63),
     (1, 64),
@@ -189,7 +189,7 @@
     (1, 65),
     (0, 40),
     (1, 66),
-    (2, ([17, 18, 19], [], [])),
+    (2, ([17, 18, 19], [], [], [])),
     (0, 46),
     (1, 67),
     (1, 68),
@@ -200,7 +200,7 @@
     (0, 50),
     (0, 48),
     (1, 70),
-    (2, ([20, 21, 22], [], [])),
+    (2, ([20, 21, 22], [], [], [])),
     (0, 51),
     (1, 71),
     (0, 54),
@@ -209,7 +209,7 @@
     (0, 52),
     (0, 55),
     (0, 53),
-    (2, ([23, 24, 25], [], [])),
+    (2, ([23, 24, 25], [], [], [])),
     (0, 57),
     (0, 61),
     (1, 73),
@@ -217,23 +217,23 @@
     (0, 58),
     (0, 60),
     (0, 59),
-    (2, ([26, 27], [], [])),
+    (2, ([26, 27], [], [], [])),
     (0, 68),
     (0, 65),
     (0, 63),
     (0, 64),
     (0, 66),
-    (2, ([28, 29], [], [])),
+    (2, ([28, 29], [(10, 1)], [], [])),
     (0, 67),
     (0, 69),
     (0, 70),
     (0, 72),
-    (2, ([30, 31, 32], [], [])),
+    (2, ([30, 31, 32], [(6, 1), (6, 2), (12, 1), (13, 0)], [], [])),
     (0, 71),
     (0, 73),
-    (2, ([33, 34, 35], [9, 0], [])),
-    (2, ([36, 37], [7, 12, 13, 10, 6], [])),
-    (2, ([38, 39], [5], [2, 8, 11, 3, 4, 1])),
+    (2, ([33, 34, 35], [(0, 0), (0, 1), (0, 2), (5, 1), (7, 1), (9, 1), (11, 0), (11, 2), (13, 1)], [], [9, 0])),
+    (2, ([36, 37], [(4, 1), (5, 0), (6, 0), (7, 0), (7, 2), (10, 0), (10, 2), (12, 0), (12, 2), (13, 2)], [], [7, 12, 13, 6, 10])),
+    (2, ([38, 39], [(3, 1), (4, 0), (5, 2), (8, 1)], [(1, 0), (1, 1), (1, 2), (2, 0), (2, 1), (2, 2), (3, 0), (3, 2), (4, 2), (8, 0), (8, 2), (11, 1)], [5, 2, 8, 11, 1, 3, 4])),
 ]
 
 
@@ -395,7 +395,7 @@
             id_copy(index, next(row_sems)).start()
 
     def step(work):
-        batch, before, after = work
+        batch, before, after, complete = work
         for index in batch:
             slot, piece, _ = STEPS[index]
             if slot not in twin_id_fresh:
@@ -405,14 +405,14 @@
 
         @pl.when(core < 2)
         def _():
-            for slot in before:
-                sum_up(slot)
+            for slot, piece in before:
+                sum_up(slot, piece)
             for index in batch:
                 compare(*STEPS[index])
-            for slot in after:
-                sum_up(slot)
-
-        for slot in before + after:
+            for slot, piece in after:
+                sum_up(slot, piece)
+
+        for slot in complete:
             for to_core in range(2 if slot else 1):
                 home_copy(slot, to_core).start()
 
@@ -456,18 +456,17 @@
         target, semaphore, device = returned.at[slot, core], home_recv.at[1], device_at(SLOTS[slot], to_core)
         return remote(partial.at[slot, to_core], target, next(row_sems), semaphore, device)
 
-    def sum_up(slot):
-        for piece in range(PIECES):
-            mine = None
-            if (slot, piece) in row_touched:
-                mine = jnp.max(row_best[slot, piece].T, axis=0, keepdims=True)
-            for half in range(2):
-                best = jnp.full((1, PIECE), NEG, jnp.float32)
-                if mine is not None:
-                    best = jnp.where(core == half, mine, best)
-                if (slot, piece) in col_touched:
-                    best = jnp.maximum(best, jnp.max(col_best[slot, piece, half], axis=0, keepdims=True))
-                partial[slot, half, :, piece * PIECE:(piece + 1) * PIECE] = best
+    def sum_up(slot, piece):
+        mine = None
+        if (slot, piece) in row_touched:
+            mine = jnp.max(row_best[slot, piece].T, axis=0, keepdims=True)
+        for half in range(2):
+            best = jnp.full((1, PIECE), NEG, jnp.float32)
+            if mine is not None:
+                best = jnp.where(core == half, mine, best)
+            if (slot, piece) in col_touched:
+                best = jnp.maximum(best, jnp.max(col_best[slot, piece, half], axis=0, keepdims=True))
+            partial[slot, half, :, piece * PIECE:(piece + 1) * PIECE] = best
 
     for kind, what in ORDER:
         if kind != 1:

time: 39.3 us -> 39.2 us (level)
  no operation moved by 1% of the time
where the time goes in v6:
time: 39.2 us; the launch traced here: 39.1 us
  Pallas kernels  37.8 us (96%)
  other arithmetic  1.28 us (3%)
    pallas_call x1, Pallas kernels, local(): pl.pallas_call(kernel, out_shape=jax.ShapeDtypeStruct((1, count), jnp.flo...  37.8 us
    pallas_call x1, other arithmetic, local(): pl.pallas_call(kernel, out_shape=jax.ShapeDtypeStruct((1, count), jnp.flo...  1.28 us

profile of v6, /device:TPU:1, one launch (start us, length us, event | category | flops | bytes accessed | tf_op | source)
XLA Modules:
  0.0 39.1 jit_solution(3815710843688059676)
XLA Ops:
  0.0 37.8 %shard_map.28 = f32[1,384]{1,0:T(1,128)} custom-call(bf16[384,512]{1,0:T(8,128)(2,1)} %x_ref.1, s32[1,384]{1,0:T(1,128)} %bitcast.1), custom_call_target="tpu_custom_call" | custom-call | tf_op jit(solution)/shard_map/pallas_call | solution.py:502
  37.8 1.3 %reduce = f32[384]{0:T(512)} reduce(f32[1,384]{1,0:T(1,128)} %shard_map.28, f32[]{:T(128)} %constant), dimensions={0}, to_apply=%pallas_call.3.reduce_sub_computation | reduce | bytes 3076 | tf_op jit(solution)/shard_map/pallas_call | solution.py:502
